TPU v7x, 256 devices: a whole 4x4x8 slice. The times are simulated.
256 devices in a mesh: row: 16 (over y, x_hi, core), col: 16 (over x_lo, z).
Axes of the slice: x: 4 (x_hi: 2, x_lo: 2; x = x_hi * 2 + x_lo), y: 4, z: 8, core: 2. Of those that a mesh axis runs over, the one named last changes fastest.
Arguments:
- patch_tokens: bfloat16 [256, 256, 3072], P('row', 'col'), may hold values from -6 to 6
- queries: bfloat16 [256, 256, 1536], P('row', 'col'), may hold values from -6 to 6
- key_vectors: bfloat16 [256, 256, 1536], P('row', 'col'), may hold values from -6 to 6
- cotangent: bfloat16 [256, 256, 1536], P('row', 'col'), may hold values from -6 to 6
- value_weight: bfloat16 [3072, 1536], P(('row', 'col')), may hold values from -0.109375 to 0.109375
- adapter_down: bfloat16 [3072, 64], replicated, may hold values from -0.109375 to 0.109375
- adapter_up: bfloat16 [64, 1536], replicated, may hold values from -0.75 to 0.75
- radius: int32 [12], replicated, may hold values from 1 to 16, as said below
- tile_mask: int32 [16, 16, 9], P('row', 'col'), may hold values from 0 to 1, as said below
Outputs:
- attended: bfloat16 [256, 256, 1536], P('row', 'col')
- grad_down: float32 [3072, 64], P(('row', 'col'))
- grad_up: float32 [64, 1536], replicated
Inputs may be any that keep to these rules, and one draw needn't show every extreme that they name: Some head has radius exactly 16. `tile_mask`: the centre entry (index 4) is 1 for every tile.
All inputs are finite; a program needn't handle non-finite values.
Results may differ from a plain program's by a relative error of at most 0.0061.
Values may be sent and summed in bfloat16 or wider, within the bound.
A program may use at most 128 MiB of HBM per device.

v0:
```python
import jax
import jax.numpy as jnp
from jax import lax
from jax.sharding import PartitionSpec as P

neg_fill = -1e30


def extended(x, sides, width):
    for axis, dim in sides:
        size, length = (lax.axis_size(axis), x.shape[dim])
        up = [(i, (i + 1) % size) for i in range(size - 1)]
        down = [(j, i) for i, j in up]
        last = lax.slice_in_dim(x, length - width, length, axis=dim)
        leading = lax.slice_in_dim(x, 0, width, axis=dim)
        before = lax.ppermute(last, axis, up)
        after = lax.ppermute(leading, axis, down)
        x = jnp.concatenate([before, x, after], axis=dim)
    return x


def shifted(block, axis, distance):
    devices = range(lax.axis_size(axis))
    route = [(i - distance, i) for i in devices if i - distance in devices]
    return lax.ppermute(block, axis, route)


def window_geometry(tile_side, row_tile, col_tile, rows_total, cols_total, mask_nine):
    window_side = 3 * tile_side
    query_pos = lax.iota(jnp.int32, tile_side * tile_side)
    query_row = query_pos // tile_side
    query_col = query_pos % tile_side
    key_pos = lax.iota(jnp.int32, window_side * window_side)
    key_row = key_pos // window_side
    key_col = key_pos % window_side
    row_gap = key_row[None, :] - tile_side - query_row[:, None]
    col_gap = key_col[None, :] - tile_side - query_col[:, None]
    distance = row_gap * row_gap + col_gap * col_gap
    global_row = row_tile * tile_side + key_row - tile_side
    global_col = col_tile * tile_side + key_col - tile_side
    in_image = (
        (global_row >= 0)
        & (global_row < rows_total)
        & (global_col >= 0)
        & (global_col < cols_total)
    )
    block_index = key_row // tile_side * 3 + key_col // tile_side
    nine = lax.iota(jnp.int32, 9)
    permitted = (
        jnp.sum(jnp.where(block_index[:, None] == nine[None, :], mask_nine[None, :], 0), axis=1) > 0
    )
    allowed = jnp.broadcast_to((in_image & permitted)[None, :], distance.shape)
    return (allowed, distance)


def window_heads(
    query_rows, key_rows, value_rows, cotangent_rows, allowed, distance, radius, head_size
):
    head_count = radius.shape[0]

    def one_head(head_index):
        offset = head_index * head_size
        query_part = lax.dynamic_slice_in_dim(query_rows, offset, head_size, 1)
        key_part = lax.dynamic_slice_in_dim(key_rows, offset, head_size, 1)
        value_part = lax.dynamic_slice_in_dim(value_rows, offset, head_size, 1)
        cotangent_part = lax.dynamic_slice_in_dim(cotangent_rows, offset, head_size, 1)
        scores = lax.dot_general(
            query_part, key_part, (((1,), (1,)), ((), ())), preferred_element_type=jnp.float32
        )
        scores = scores * head_size ** (-0.5)
        inside = allowed & (distance <= radius[head_index] * radius[head_index])
        scores = jnp.where(inside, scores, neg_fill)
        row_max = jnp.max(scores, axis=1, keepdims=True)
        unnormed = jnp.where(inside, jnp.exp(scores - row_max), 0.0)
        weights = (unnormed / jnp.sum(unnormed, axis=1, keepdims=True)).astype(jnp.bfloat16)
        head_out = jnp.dot(weights, value_part, preferred_element_type=jnp.float32).astype(
            jnp.bfloat16
        )
        head_grad = lax.dot_general(
            weights, cotangent_part, (((0,), (0,)), ((), ())), preferred_element_type=jnp.float32
        ).astype(jnp.bfloat16)
        return (head_out, head_grad)

    outputs, grads = lax.map(one_head, jnp.arange(head_count, dtype=jnp.int32))
    outputs = outputs.transpose(1, 0, 2).reshape(query_rows.shape[0], head_count * head_size)
    grads = grads.transpose(1, 0, 2).reshape(key_rows.shape[0], head_count * head_size)
    return (outputs, grads)


def per_device(
    patch_tokens,
    queries,
    key_vectors,
    cotangent,
    value_weight,
    adapter_down,
    adapter_up,
    radius,
    tile_mask,
):
    tile_side = patch_tokens.shape[0]
    width = patch_tokens.shape[2]
    rank = adapter_down.shape[1]
    inner = adapter_up.shape[1]
    head_size = inner // radius.shape[0]
    flat_tokens = patch_tokens.reshape(tile_side * tile_side, width)
    lowrank = jnp.dot(flat_tokens, adapter_down, preferred_element_type=jnp.float32).astype(
        jnp.bfloat16
    )
    frozen = jnp.dot(
        flat_tokens,
        lax.all_gather(value_weight, ("row", "col"), axis=0, tiled=True),
        preferred_element_type=jnp.float32,
    )
    values = (frozen + jnp.dot(lowrank, adapter_up, preferred_element_type=jnp.float32)).astype(
        jnp.bfloat16
    )
    packed = jnp.concatenate(
        [
            key_vectors,
            values.reshape(tile_side, tile_side, inner),
            lowrank.reshape(tile_side, tile_side, rank),
        ],
        axis=2,
    )
    window = extended(packed, (("row", 0), ("col", 1)), tile_side)
    window = window.reshape(9 * tile_side * tile_side, 2 * inner + rank)
    rows_total = tile_side * lax.axis_size("row")
    cols_total = tile_side * lax.axis_size("col")
    allowed, distance = window_geometry(
        tile_side,
        lax.axis_index("row"),
        lax.axis_index("col"),
        rows_total,
        cols_total,
        tile_mask.reshape(9),
    )
    attended, value_grad = window_heads(
        queries.reshape(tile_side * tile_side, inner),
        window[:, :inner],
        window[:, inner : 2 * inner],
        cotangent.reshape(tile_side * tile_side, inner),
        allowed,
        distance,
        radius,
        head_size,
    )
    up_term = lax.dot_general(
        window[:, 2 * inner :],
        value_grad,
        (((0,), (0,)), ((), ())),
        preferred_element_type=jnp.float32,
    )
    back_window = lax.dot_general(
        value_grad, adapter_up, (((1,), (1,)), ((), ())), preferred_element_type=jnp.float32
    )
    blocks = back_window.reshape(3, tile_side, 3, tile_side, rank)
    middle = blocks[1]
    for step_by, outgoing in ((1, blocks[2]), (-1, blocks[0])):
        middle = middle + shifted(outgoing.astype(jnp.bfloat16), "row", step_by).astype(
            outgoing.dtype
        )
    back = middle[:, 1]
    for step_by, outgoing in ((1, middle[:, 2]), (-1, middle[:, 0])):
        back = back + shifted(outgoing.astype(jnp.bfloat16), "col", step_by).astype(outgoing.dtype)
    device_count = lax.axis_size("row") * lax.axis_size("col")
    scale = (tile_side * tile_side * device_count) ** (-0.5)
    down_term = lax.dot_general(
        flat_tokens.astype(jnp.float32),
        back.reshape(tile_side * tile_side, rank),
        (((0,), (0,)), ((), ())),
        precision=lax.Precision.HIGHEST,
    )
    grad_down = lax.psum_scatter(down_term, ("row", "col"), scatter_dimension=0, tiled=True)
    up_all = lax.psum(up_term, ("row", "col"))
    return (attended.reshape(tile_side, tile_side, inner), grad_down * scale, up_all * scale)


def solution(mesh):
    placed = (
        P("row", "col", None),
        P("row", "col", None),
        P("row", "col", None),
        P("row", "col", None),
        P(("row", "col"), None),
        P(),
        P(),
        P(),
        P("row", "col", None),
    )
    return jax.shard_map(
        per_device,
        mesh=mesh,
        in_specs=placed,
        out_specs=(P("row", "col", None), P(("row", "col"), None), P()),
        check_vma=False,
    )
```

profile of v0, /device:TPU:1, one launch (start us, length us, event | category | flops | bytes accessed | tf_op | source)
XLA Modules:
  0.0 1428.7 jit_solution(13788041792475653919)
XLA Ops:
  10.3 729.8 %all-gather.3.cloned.1.call-done = bf16[256,12,1536]{2,1,0:T(8,128)(2,1)} async-done(((bf16[1,12,1536]{2,1,0:T(8,128)(2,1)}), bf16[256,12,1536]{2,1,0:T(8,128)(2,1)}) %all-gather.3.cloned.1.call-update) | async-done | bytes 9437200 | tf_op jit(solution)/shard_map/all_gather | solution.py:112
  740.1 15.0 %reshape.162 = bf16[3072,1536]{1,0:T(8,128)(2,1)} reshape(bf16[256,12,1536]{2,1,0:T(8,128)(2,1)} %all-gather.3.cloned.1.call-done) | data formatting | bytes 18874368
  755.1 5.2 fusion.56
  761.6 2.8 collective-permute-start.1
  764.4 4.2 collective-permute-start
  768.7 34.0 %collective-permute-done.1 = bf16[16,16,3136]{2,1,0:T(8,128)(2,1)S(1)} collective-permute-done((bf16[16,16,3136]{2,1,0:T(8,128)(2,1)S(1)}, bf16[16,16,3136]{2,1,0:T(8,128)(2,1)S(1)}, u32[]{:S(2)}, u32[]{:S(2)}) %collective-permute-start.1) | collective-permute-done | bytes 1605664 | tf_op jit(solution)/shard_map/ppermute | solution.py:17
  802.6 10.5 pad_maximum_fusion.1
  814.4 6.2 collective-permute-start.2
  820.8 70.7 %collective-permute-done.3 = bf16[48,16,3136]{2,1,0:T(8,128)(2,1)} collective-permute-done((bf16[48,16,3136]{2,1,0:T(8,128)(2,1)}, bf16[48,16,3136]{2,1,0:T(8,128)(2,1)}, u32[]{:S(2)}, u32[]{:S(2)}) %collective-permute-start.3) | collective-permute-done | bytes 4816928 | tf_op jit(solution)/shard_map/ppermute | solution.py:17
  891.6 1.8 collective-permute-done.2
  893.3 15.3 %pad_maximum_fusion = bf16[48,48,3136]{2,1,0:T(8,128)(2,1)S(1)} fusion(bf16[48,16,3136]{2,1,0:T(8,128)(2,1)} %collective-permute-done.3, bf16[16,16,3136]{2,1,0:T(8,128)(2,1)} %copy-done.3, bf16[16,16,64]{2,1,0:T(8,128)(2,1)S(1)} %bitcast.80, bf16[16,16,1536]{2,1,0:T(8,128)(2,1)S(1)} %bitcast.76, bf16[16,16,1536]{2,1,0:T(8,128)(2,1)S(1)} %copy-done.2, ...), kind=kLoop, calls=%fused_computation.22 | loop fusion | flops 101154816 | bytes 28901376 | tf_op jit(solution)/shard_map/concatenate | solution.py:18
  908.6 6.3 fusion.53
  914.9 3.1 copy-done.1
  918.0 178.6 %while.13 = (s32[]{:T(128)}, bf16[12,256,128]{2,1,0:T(8,128)(2,1)}, bf16[12,2304,128]{1,2,0:T(8,128)(2,1)}, s32[12]{0:T(128)S(1)}, s32[12]{0:T(128)S(1)}, /*inde...) while((s32[]{:T(128)}, bf16[12,256,128]{2,1,0:T(8,128)(2,1)}, ...), condition=%wide.region_4.5_spmd.clone, body=%wide.region_1.4_spmd.clone.sunk | while | flops 471596544 | bytes 15017537 | solution.py:84
  923.1 2.3 fusion.81
  928.3 2.2 fusion.83
  938.0 2.3 fusion.81
  943.1 2.2 fusion.83
  952.9 2.3 fusion.81
  956.4 1.6 divide_convert_fusion.2
  958.0 2.2 fusion.83
  967.7 2.3 fusion.81
  972.9 2.2 fusion.83
  982.6 2.3 fusion.81
  987.8 2.2 fusion.83
  997.5 2.3 fusion.81
  1002.6 2.2 fusion.83
  1012.4 2.3 fusion.81
  1017.5 2.2 fusion.83
  1027.3 2.3 fusion.81
  1032.4 2.2 fusion.83
  1042.1 2.3 fusion.81
  1047.3 2.2 fusion.83
  1057.0 2.3 fusion.81
  1062.2 2.2 fusion.83
  1071.9 2.3 fusion.81
  1077.0 2.2 fusion.83
  1086.8 2.3 fusion.81
  1091.9 2.2 fusion.83
  1096.6 4.4 fusion.55
  1101.1 1.9 collective-permute-start.5
  1103.2 32.6 %collective-permute-start.4 = (bf16[16,3,16,64]{3,2,1,0:T(8,128)(2,1)S(1)}, bf16[16,3,16,64]{3,2,1,0:T(8,128)(2,1)S(1)}, u32[]{:S(2)}, u32[]{:S(2)}) collective-permute-start(bf16[16,3,16,64]{3,2,1,0:T(8,128)(2,1)S(1)} %bitcast.82), channel_id=1, source_target_pairs={{0,16},{16,32},{32,48},{48,64},{64,80},{80,96},{96,112},{112,128},... | collective-permute-start | bytes 294920 | tf_op jit(solution)/shard_map/ppermute | solution.py:25
  1139.8 4.9 collective-permute-start.6
  1144.7 6.2 fusion.18
  1151.0 1.9 convolution_bitcast_fusion
  1152.9 1.7 copy.37
  1156.0 262.5 %all-reduce.4.cloned.1.call-done = (f32[3072,64]{0,1:T(8,128)}, f32[64,1536]{1,0:T(8,128)}) async-done(((f32[3072,64]{0,1:T(8,128)}, f32[64,1536]{1,0:T(8,128)}), (f32[3072,64]{0,1:T(8,128)}, f32[64,1536]{1,0:T(8,128)})) %all-reduce.4.cloned.1.call-update) | async-done | bytes 1179664
  1420.1 1.8 broadcast_multiply_fusion
  (131 shorter events, 89.6 us)
Async XLA Ops:
  7.2 1.4 copy-start
  7.2 732.9 %all-gather.3.cloned.1.call-start = ((), (), s32[]{:S(2)}) async-start(), calls=%async_computation | async-start | bytes 12632064 | tf_op jit(solution)/shard_map/all_gather | solution.py:112
  7.9 1410.6 %all-reduce.4.cloned.1.call-start = ((), (), s32[]{:S(2)}) async-start(), calls=%async_computation.1 | async-start | bytes 2359296
  755.1 5.2 copy-start.5
  760.3 1.1 copy-start.2
  761.6 59.1 %copy-start.6 = (s32[1,1,9]{2,1,0:T(1,128)S(1)}, s32[1,1,9]{2,1,0:T(1,128)}, u32[]{:S(2)}) copy-start(s32[1,1,9]{2,1,0:T(1,128)} %param.19) | copy-start | bytes 112
  761.6 41.1 %collective-permute-start.1 = (bf16[16,16,3136]{2,1,0:T(8,128)(2,1)S(1)}, bf16[16,16,3136]{2,1,0:T(8,128)(2,1)S(1)}, u32[]{:S(2)}, u32[]{:S(2)}) collective-permute-start(bf16[16,16,3136]{2,1,0:T(8,128)(2,1)S(1)} %pad_maximum_fusion.2), channel_id=1, source_target_pairs={{16,0},{32,16},{48,32},{64,48},{80,64},{96,80},{112,96},{128,112},... | collective-permute-start | bytes 4816904 | tf_op jit(solution)/shard_map/ppermute | solution.py:17
  764.4 38.2 %collective-permute-start = (bf16[16,16,3136]{2,1,0:T(8,128)(2,1)S(1)}, bf16[16,16,3136]{2,1,0:T(8,128)(2,1)S(1)}, u32[]{:S(2)}, u32[]{:S(2)}) collective-permute-start(bf16[16,16,3136]{2,1,0:T(8,128)(2,1)S(1)} %pad_maximum_fusion.2), channel_id=1, source_target_pairs={{0,16},{16,32},{32,48},{48,64},{64,80},{80,96},{96,112},{112,128},... | collective-permute-start | bytes 4816904 | tf_op jit(solution)/shard_map/ppermute | solution.py:16
  802.6 10.5 copy-start.3
  802.6 10.5 copy-start.4
  813.1 78.4 %collective-permute-start.3 = (bf16[48,16,3136]{2,1,0:T(8,128)(2,1)}, bf16[48,16,3136]{2,1,0:T(8,128)(2,1)}, u32[]{:S(2)}, u32[]{:S(2)}) collective-permute-start(bf16[48,16,3136]{2,1,0:T(8,128)(2,1)} %pad_maximum_fusion.1), channel_id=1, source_target_pairs={{1,0},{2,1},{3,2},{4,3},{5,4},{6,5},{7,6},{8,7},{9,8},{10,9},{11,1... | collective-permute-start | bytes 14450696 | tf_op jit(solution)/shard_map/ppermute | solution.py:17
  814.4 78.9 %collective-permute-start.2 = (bf16[48,16,3136]{2,1,0:T(8,128)(2,1)}, bf16[48,16,3136]{2,1,0:T(8,128)(2,1)}, u32[]{:S(2)}, u32[]{:S(2)}) collective-permute-start(bf16[48,16,3136]{2,1,0:T(8,128)(2,1)} %pad_maximum_fusion.1), channel_id=1, source_target_pairs={{0,1},{1,2},{2,3},{3,4},{4,5},{5,6},{6,7},{7,8},{8,9},{9,10},{10,1... | collective-permute-start | bytes 14450696 | tf_op jit(solution)/shard_map/ppermute | solution.py:16
  908.6 9.5 copy-start.1
  908.6 9.5 copy-start.7
  1101.1 35.9 %collective-permute-start.5 = (bf16[16,3,16,64]{3,2,1,0:T(8,128)(2,1)S(1)}, bf16[16,3,16,64]{3,2,1,0:T(8,128)(2,1)S(1)}, u32[]{:S(2)}, u32[]{:S(2)}) collective-permute-start(bf16[16,3,16,64]{3,2,1,0:T(8,128)(2,1)S(1)} %bitcast.81), channel_id=1, source_target_pairs={{16,0},{32,16},{48,32},{64,48},{80,64},{96,80},{112,96},{128,112},... | collective-permute-start | bytes 294920 | tf_op jit(solution)/shard_map/ppermute | solution.py:25
  1103.2 35.2 %collective-permute-start.4 = (bf16[16,3,16,64]{3,2,1,0:T(8,128)(2,1)S(1)}, bf16[16,3,16,64]{3,2,1,0:T(8,128)(2,1)S(1)}, u32[]{:S(2)}, u32[]{:S(2)}) collective-permute-start(bf16[16,3,16,64]{3,2,1,0:T(8,128)(2,1)S(1)} %bitcast.82), channel_id=1, source_target_pairs={{0,16},{16,32},{32,48},{48,64},{64,80},{80,96},{96,112},{112,128},... | collective-permute-start | bytes 294920 | tf_op jit(solution)/shard_map/ppermute | solution.py:25
  1138.5 12.5 collective-permute-start.7
  1139.8 11.2 collective-permute-start.6
Sparse Core Ops, SparseCore 0:
  9.9 730.1 all-gather.2
  1153.0 265.4 all-reduce.3
where the time goes:
time: 1430 us
  waiting for transfers between devices  1100 us (77%)
  matrix products  89.5 us (6%)
  other arithmetic  63.1 us (4%)
  local copies, waits for them, and re-layouts  57.6 us (4%)
  starting transfers between devices  55.3 us (4%)
  loops' own time  47 us (3%)
  between operations  14.3 us (1%)
    all_gather x1, waiting for transfers between devices, per_device(): lax.all_gather(value_weight, ('row', 'col'), axis=0, tiled=True)  730 us
    unnamed x3, waiting for transfers between devices  263 us
    ppermute x2, waiting for transfers between devices, extended(): after = lax.ppermute(leading, axis, down)  105 us
    another operation x1, loops' own time, window_heads(): outputs, grads = lax.map(one_head, jnp.arange(head_count, dtype=jnp.int32))  47 us
    ppermute x4, starting transfers between devices, shifted(): return lax.ppermute(block, axis, route)  40.7 us
  transfers between devices with their start and end apart: 10, of which 7 were waited for; matrix products, arithmetic and copies ran while one was open for 1% of the time, Pallas kernels for 0%

commit v1 on v0

v1 whole, which is shorter than its diff:
```python
import functools

import jax
import jax.numpy as jnp
import numpy as np
from jax import lax
from jax.experimental import pallas as pl
from jax.experimental.pallas import tpu as pltpu
from jax.sharding import PartitionSpec as P

MESH = pl.DeviceIdType.MESH
BF = jnp.bfloat16
F32 = jnp.float32
HALF = 768
MIB = 2**20


def place():
    row = lax.axis_index("row")
    col = lax.axis_index("col")
    return row, col


def grid_place():
    row, col = place()
    y = lax.div(row, 4)
    x = lax.rem(lax.div(row, 2), 2) * 2 + lax.div(col, 8)
    return y, x, lax.rem(col, 8), lax.rem(row, 2)


def at_grid(y, x, z, c):
    y = lax.rem(y + 4, 4)
    x = lax.rem(x + 4, 4)
    z = lax.rem(z + 8, 8)
    return (y * 4 + lax.div(x, 2) * 2 + c, lax.rem(x, 2) * 8 + z)


def at_chip(k, h, col):
    return (lax.rem(k + 8, 8) * 2 + h, lax.rem(col + 16, 16))


def greet(targets):
    barrier = pltpu.get_barrier_semaphore()
    for target in targets:
        pl.semaphore_signal(barrier, inc=1, device_id=target, device_id_type=MESH)
    pl.semaphore_wait(barrier, len(targets))


class Wire:
    def __init__(self, send, recv):
        self.send, self.recv, self.pending = send, recv, []

    def copy(self, src, dst, target, s, r):
        return pltpu.make_async_remote_copy(
            src_ref=src,
            dst_ref=dst,
            send_sem=self.send.at[s],
            recv_sem=self.recv.at[r],
            device_id=target,
            device_id_type=MESH,
        )

    def start(self, src, dst, target, s, r):
        copy = self.copy(src, dst, target, s, r)
        copy.start()
        self.pending.append(copy)

    def arrived(self, dst, r):
        row, col = place()
        self.copy(dst, dst, (row + 1 - 2 * lax.rem(row, 2), col), r, r).wait_recv()

    def drain(self):
        for copy in self.pending:
            copy.wait_send()
        self.pending = []


def chip_targets():
    row, col = place()
    k, c = lax.div(row, 2), lax.rem(row, 2)
    out = [at_chip(k, 1 - c, col)]
    for h in (0, 1):
        out += [at_chip(k + 1, h, col), at_chip(k - 1, h, col)]
        out += [at_chip(k, h, col + 1), at_chip(k, h, col - 1)]
    return out


def stretch(c):
    return pl.multiple_of(c * HALF, HALF)


def gather_kernel(
    q, kv, cot, x, low, wp, allow, q2, kwin, c2, lwin, x2, wout, allow2, zbuf, wblk, send, recv, local
):
    row, col = place()
    k, c = lax.div(row, 2), lax.rem(row, 2)
    y, xx, z, _ = grid_place()
    other = 1 - c
    mine = stretch(c)
    wire = Wire(send, recv)
    targets = chip_targets()
    for a in range(1, 8):
        targets += [at_grid(y, xx, z + a, 0), at_grid(y, xx, z + a, 1)]
    targets += [at_grid(y + 1, xx, z, c), at_grid(y - 1, xx, z, c)]
    targets += [at_grid(y, xx + 1, z, c), at_grid(y, xx - 1, z, c)]
    greet(targets)
    sib = at_chip(k, other, col)
    theirs = stretch(other)

    locals_ = []

    def local_copy(src, dst):
        copy = pltpu.make_async_copy(src, dst, local.at[len(locals_)])
        copy.start()
        locals_.append(copy)
        return copy

    slot = c * 8 + z
    own_w = local_copy(wp.at[:, pl.ds(mine, HALF)], zbuf.at[slot])
    wire.start(wp.at[:, pl.ds(theirs, HALF)], zbuf.at[slot], sib, 0, 0)
    for a in range(1, 8):
        for h in (0, 1):
            hh = c if h == 0 else other
            wire.start(
                wp.at[:, pl.ds(stretch(hh), HALF)],
                zbuf.at[slot],
                at_grid(y, xx, z + a, hh),
                2 * a + h,
                2 * a + h,
            )
    far = (3 - 3 * c) * 3 + 1
    up = 2 * c - 1
    for h in (0, 1):
        part = kv.at[:, pl.ds(h * HALF, HALF)]
        wire.start(part, kwin.at[far], at_chip(k + up, h, col), 16 + h, 16 + c)
        wire.start(low, lwin.at[far], at_chip(k + up, h, col), 18 + h, 18 + c)
    for h in (0, 1):
        part = kv.at[:, pl.ds(h * HALF, HALF)]
        for i, d in enumerate((1, -1)):
            wire.start(
                part, kwin.at[(1 + c) * 3 + 1 - d], at_chip(k, h, col + d), 20 + 2 * i + h, 20 + 2 * i + c
            )
            wire.start(
                low, lwin.at[(1 + c) * 3 + 1 - d], at_chip(k, h, col + d), 24 + 2 * i + h, 24 + 2 * i + c
            )
    centre = (1 + c) * 3 + 1
    wire.start(kv.at[:, pl.ds(theirs, HALF)], kwin.at[centre], sib, 28, 28)
    wire.start(low, lwin.at[centre], sib, 29, 29)
    wire.start(q.at[:, pl.ds(theirs, HALF)], q2.at[c], sib, 30, 30)
    wire.start(cot.at[:, pl.ds(theirs, HALF)], c2.at[c], sib, 31, 31)
    wire.start(x, x2.at[c], sib, 32, 32)
    wire.start(allow, allow2.at[c], sib, 33, 33)
    local_copy(kv.at[:, pl.ds(mine, HALF)], kwin.at[centre])
    local_copy(low, lwin.at[centre])
    local_copy(q.at[:, pl.ds(mine, HALF)], q2.at[c])
    local_copy(cot.at[:, pl.ds(mine, HALF)], c2.at[c])
    local_copy(x, x2.at[c])
    local_copy(allow, allow2.at[c])

    own_w.wait()
    wire.arrived(zbuf.at[0], 0)
    for a in range(1, 8):
        for h in (0, 1):
            wire.arrived(zbuf.at[0], 2 * a + h)
    r_out = lax.broadcasted_iota(jnp.int32, (96, 128), 0)
    r_in = lax.broadcasted_iota(jnp.int32, (96, 128), 1)
    pick = jnp.where(lax.div(r_out, 12) * 16 + lax.rem(r_out, 12) == r_in, 1.0, 0.0).astype(BF)
    for cc in (0, 1):
        part = zbuf[pl.ds(cc * 8, 8)].reshape(128, HALF)
        wblk[cc] = jnp.dot(pick, part, preferred_element_type=F32).astype(BF)

    xs = (at_grid(y, xx + 1, z, c), at_grid(y, xx - 1, z, c))
    ys = (at_grid(y + 1, xx, z, c), at_grid(y - 1, xx, z, c))

    def x_part(i):
        i = lax.rem(i + 4, 4)
        return lax.div(i, 2), lax.rem(i, 2)

    def y_part(i):
        return lax.rem(i + 4, 4)

    def small(yi, xi):
        a, b = x_part(xi)
        return wout.at[y_part(yi), a, :, b]

    def small_half(yi, xi, j):
        a, b = x_part(xi)
        return wout.at[y_part(yi), a, j, b]

    def strip(xi):
        a, b = x_part(xi)
        return wout.at[:, a, :, b]

    def strip_half(xi, j):
        a, b = x_part(xi)
        return wout.at[:, a, j, b]

    own_copy = pltpu.make_async_copy(wblk, small(y, xx), local.at[7])
    own_copy.start()

    def corners(wire):
        wire.arrived(kwin.at[1], 17)
        wire.arrived(lwin.at[1], 19)
        wire.arrived(kwin.at[10], 16)
        wire.arrived(lwin.at[10], 18)
        n = 44
        for rr in (0, 3):
            for d in (1, -1):
                dst = rr * 3 + 1 - d
                target = at_chip(k, c, col + d)
                wire.start(kwin.at[rr * 3 + 1], kwin.at[dst], target, n, n)
                wire.start(lwin.at[rr * 3 + 1], lwin.at[dst], target, n + 1, n + 1)
                n += 2

    def ring(wire, index, block, half, n, targets, src):
        nxt, prv = targets
        wire.start(src, block(index), nxt, n, n)
        wire.start(src, block(index), prv, n + 1, n + 1)

        def second():
            wire.arrived(block(index), n)
            wire.start(half(index - 1, 0), half(index - 1, 0), nxt, n + 2, n + 2)
            wire.arrived(block(index), n + 1)
            wire.start(half(index + 1, 1), half(index + 1, 1), prv, n + 3, n + 3)

        def last():
            wire.arrived(half(index, 0), n + 2)
            wire.arrived(half(index, 1), n + 3)

        return second, last

    def spread(along_x):
        sub = Wire(send, recv)
        x_small = (xx, lambda i: small(y, i), lambda i, j: small_half(y, i, j))
        y_small = (y, lambda i: small(i, xx), lambda i, j: small_half(i, xx, j))
        x_big = (xx, strip, strip_half)
        y_big = (y, lambda i: wout.at[y_part(i)], lambda i, j: wout.at[y_part(i), j])
        one, two = (x_small, y_big) if along_x else (y_small, x_big)
        first_to, second_to = (xs, ys) if along_x else (ys, xs)
        second, last = ring(sub, *one, 34, first_to, wblk)
        second()
        corners(sub)
        last()
        own_copy.wait()
        second, last = ring(sub, *two, 38, second_to, two[1](two[0]))
        second()
        last()
        sub.drain()

    @pl.when(c == 0)
    def _():
        spread(True)

    @pl.when(c == 1)
    def _():
        spread(False)

    for cc in (0, 1):
        for i in (0, 1):
            wire.arrived(kwin.at[0], 20 + 2 * i + cc)
            wire.arrived(lwin.at[0], 24 + 2 * i + cc)
    wire.arrived(kwin.at[0], 28)
    wire.arrived(lwin.at[0], 29)
    wire.arrived(q2.at[0], 30)
    wire.arrived(c2.at[0], 31)
    wire.arrived(x2.at[0], 32)
    wire.arrived(allow2.at[0], 33)
    for n in range(44, 52, 2):
        wire.arrived(kwin.at[0], n)
        wire.arrived(lwin.at[0], n + 1)
    for copy in locals_[1:]:
        copy.wait()
    wire.drain()


def any_spec(n):
    return [pl.BlockSpec(memory_space=pl.ANY)] * n


def gather(q, kv, cot, x, low, wp, allow):
    return pl.pallas_call(
        gather_kernel,
        out_shape=[
            jax.ShapeDtypeStruct((2, 256, HALF), BF),
            jax.ShapeDtypeStruct((12, 256, HALF), BF),
            jax.ShapeDtypeStruct((2, 256, HALF), BF),
            jax.ShapeDtypeStruct((12, 256, 128), BF),
            jax.ShapeDtypeStruct((2, 256, 3072), BF),
            jax.ShapeDtypeStruct((4, 2, 2, 2, 96, HALF), BF),
            jax.ShapeDtypeStruct((2,) + allow.shape, F32),
        ],
        in_specs=any_spec(7),
        out_specs=any_spec(7),
        scratch_shapes=[
            pltpu.VMEM((16, 16, HALF), BF),
            pltpu.VMEM((2, 96, HALF), BF),
            pltpu.SemaphoreType.DMA((52,)),
            pltpu.SemaphoreType.DMA((52,)),
            pltpu.SemaphoreType.DMA((8,)),
        ],
        compiler_params=pltpu.CompilerParams(collective_id=0, has_side_effects=True),
        name="gather",
    )(q, kv, cot, x, low, wp, allow)


def halo_kernel(v, vwin, send, recv, local):
    row, col = place()
    k, c = lax.div(row, 2), lax.rem(row, 2)
    wire = Wire(send, recv)
    up, down = at_chip(k - 1, c, col), at_chip(k + 1, c, col)
    sides = [at_chip(k, c, col + d) for d in (1, -1)]
    greet([up, down] + sides)
    wire.start(v.at[0], vwin.at[10], up, 0, 0)
    wire.start(v.at[1], vwin.at[1], down, 1, 1)
    for i, d in enumerate((1, -1)):
        for t in (0, 1):
            wire.start(v.at[t], vwin.at[(1 + t) * 3 + 1 - d], sides[i], 2 + 2 * i + t, 2 + 2 * i + t)
    copies = [pltpu.make_async_copy(v.at[t], vwin.at[4 + 3 * t], local.at[t]) for t in (0, 1)]
    for copy in copies:
        copy.start()
    n = 6
    for rr in (3, 0):
        wire.arrived(vwin.at[rr * 3 + 1], 0 if rr else 1)
        for i, d in enumerate((1, -1)):
            wire.start(vwin.at[rr * 3 + 1], vwin.at[rr * 3 + 1 - d], sides[i], n, n)
            n += 1
    for n in range(2, 10):
        wire.arrived(vwin.at[0], n)
    for copy in copies:
        copy.wait()
    wire.drain()


def halo(v):
    return pl.pallas_call(
        halo_kernel,
        out_shape=jax.ShapeDtypeStruct((12, 256, HALF), BF),
        in_specs=any_spec(1),
        out_specs=any_spec(1)[0],
        scratch_shapes=[
            pltpu.SemaphoreType.DMA((10,)),
            pltpu.SemaphoreType.DMA((10,)),
            pltpu.SemaphoreType.DMA((2,)),
        ],
        compiler_params=pltpu.CompilerParams(collective_id=1, has_side_effects=True),
        name="halo",
    )(v)


def attention_kernel(radius, q, kw, vw, cot, low, up, dist, allow, att, back, upt, s_ref, p_ref):
    h, t = pl.program_id(0), pl.program_id(1)
    keys = kw[pl.ds(t * 3, 9)].reshape(2304, 128)
    s_ref[...] = lax.dot_general(
        q[0], keys, (((1,), (1,)), ((), ())), preferred_element_type=F32
    )
    limit = allow[0, 0:1, :] * (radius[h] * radius[h] + 1.0) - 1.0
    scale = 128**-0.5

    @pl.loop(0, 8)
    def _(i):
        rows = pl.ds(pl.multiple_of(i * 32, 32), 32)
        s = jnp.where(dist[rows] <= limit, s_ref[rows] * scale, -1e30)
        e = jnp.exp(s - jnp.max(s, axis=1, keepdims=True))
        p_ref[rows] = (e * (1.0 / jnp.sum(e, axis=1, keepdims=True))).astype(BF)

    p = p_ref[...]
    vals = vw[pl.ds(t * 3, 9)].reshape(2304, 128)
    att[0] = jnp.dot(p, vals, preferred_element_type=F32).astype(BF)
    vgt = jnp.dot(cot[0].T, p, preferred_element_type=F32).astype(BF)

    @pl.when((h == 0) & (t == 0))
    def _():
        back[...] = jnp.zeros_like(back)

    bt = jnp.dot(up[...], vgt, preferred_element_type=F32)
    for n in range(9):
        back[t * 3 + n] += bt[:, n * 256 : (n + 1) * 256]
    lows = low[pl.ds(t * 3, 9)].reshape(2304, 128)
    ut = jnp.dot(vgt, lows, preferred_element_type=F32)

    @pl.when(t == 0)
    def _():
        upt[...] = ut

    @pl.when(t == 1)
    def _():
        upt[...] += ut


def distances():
    qp = np.arange(256)
    kp = np.arange(2304)
    kr = (kp // 768) * 16 + (kp % 256) // 16 - 16
    kc = (kp // 256 % 3) * 16 + kp % 16 - 16
    dr = kr[None] - (qp // 16)[:, None]
    dc = kc[None] - (qp % 16)[:, None]
    return (dr * dr + dc * dc).astype(np.float32)


def attention(radius, q2, kwin, vwin, c2, lwin, up, dist, allow2):
    return pl.pallas_call(
        attention_kernel,
        grid=(6, 2),
        out_shape=[
            jax.ShapeDtypeStruct((2, 256, HALF), BF),
            jax.ShapeDtypeStruct((12, 64, 256), F32),
            jax.ShapeDtypeStruct((HALF, 128), F32),
        ],
        in_specs=[
            pl.BlockSpec(memory_space=pltpu.SMEM),
            pl.BlockSpec((1, 256, 128), lambda h, t: (t, 0, h)),
            pl.BlockSpec((12, 256, 128), lambda h, t: (0, 0, h)),
            pl.BlockSpec((12, 256, 128), lambda h, t: (0, 0, h)),
            pl.BlockSpec((1, 256, 128), lambda h, t: (t, 0, h)),
            pl.BlockSpec((12, 256, 128), lambda h, t: (0, 0, 0)),
            pl.BlockSpec((64, 128), lambda h, t: (0, h)),
            pl.BlockSpec((256, 2304), lambda h, t: (0, 0)),
            pl.BlockSpec((1, 8, 2304), lambda h, t: (t, 0, 0)),
        ],
        out_specs=[
            pl.BlockSpec((1, 256, 128), lambda h, t: (t, 0, h)),
            pl.BlockSpec((12, 64, 256), lambda h, t: (0, 0, 0)),
            pl.BlockSpec((128, 128), lambda h, t: (h, 0)),
        ],
        scratch_shapes=[pltpu.VMEM((256, 2304), F32), pltpu.VMEM((256, 2304), BF)],
        compiler_params=pltpu.CompilerParams(vmem_limit_bytes=48 * MIB),
        name="attention",
    )(radius, q2, kwin, vwin, c2, lwin, up, dist, allow2)


def reduce_kernel(
    att_in, back, upt, x, att, gd, gu, bs, br, gs, gr, keep, xs_, xr, ys_, yr, zs, zr, send, recv, local
):
    row, col = place()
    k, c = lax.div(row, 2), lax.rem(row, 2)
    other = 1 - c
    y, xx, z, _ = grid_place()
    wire = Wire(send, recv)
    sib = at_chip(k, other, col)
    mine = stretch(c)
    xt = [at_grid(y, xx + a, z, c) for a in (1, 2, 3)]
    yt = [at_grid(y + a, xx, z, c) for a in (1, 2, 3)]
    zt = [at_grid(y, xx, z + a, c) for a in range(1, 8)]
    targets = [sib] + xt + yt + zt
    around = [(rr, cc) for rr in range(4) for cc in range(3)]
    for h in (0, 1):
        for d in (1, 0, -1):
            targets += [at_chip(k + 1, h, col + d), at_chip(k - 1, h, col + d)]
            if d:
                targets.append(at_chip(k, h, col + d))
    greet(targets)
    wire.start(att_in.at[other], att.at[:, pl.ds(mine, HALF)], sib, 0, 0)
    keep_att = pltpu.make_async_copy(att_in.at[c], att.at[:, pl.ds(mine, HALF)], local.at[0])
    keep_att.start()

    for n, (rr, cc) in enumerate(around):
        bs[n] = back[n].astype(BF)
    for n, (rr, cc) in enumerate(around):
        dk, h = ((-1, 1), (0, 0), (0, 1), (1, 0))[rr]
        adj = 0 if rr in (1, 2) else 1
        slot = adj * 6 + cc * 2
        if (rr, cc) in ((1, 1), (2, 1)):
            @pl.when(c != h)
            def _():
                copy = wire.copy(bs.at[n], br.at[slot + c], sib, 1, 2 + slot + c)
                copy.start()
                copy.wait_send()
        else:
            wire.start(
                bs.at[n], br.at[slot + c], at_chip(k + dk, h, col + cc - 1), 2 + n, 2 + slot + c
            )
    total = back[(1 + c) * 3 + 1]
    wire.arrived(br.at[0], 2 + 2 + other)
    total = total + br[2 + other].astype(F32)
    for slot in range(12):
        if slot not in (2, 3):
            wire.arrived(br.at[0], 2 + slot)
            total = total + br[slot].astype(F32)
    hi = total.astype(BF)
    lo = (total - hi.astype(F32)).astype(BF)
    both = jnp.concatenate([hi, lo], axis=0)

    @pl.loop(0, 8)
    def _(i):
        part = x[:, pl.ds(pl.multiple_of(i * 384, 384), 384)]
        g = jnp.dot(both, part, preferred_element_type=F32)
        g = (g[:64] + g[64:]).T
        yi, xhi = lax.div(i, 2), lax.rem(i, 2)
        for cc in (0, 1):
            for xl in (0, 1):
                rows = g[(cc * 2 + xl) * 96 : (cc * 2 + xl + 1) * 96]
                keep[cc, xhi * 2 + xl, yi] = rows
                gs[cc, xhi * 2 + xl, yi] = rows.astype(BF)

    wire.start(gs.at[other], gr, sib, 14, 14)
    wire.arrived(gr, 14)
    for a in range(4):
        for b in range(4):
            full = keep[c, a, b] + gr[a, b].astype(F32)
            keep[0, a, b] = full
            xs_[a, b, 0:96] = full.astype(BF)
            xs_[a, b, 96:144] = upt[a * 4 + b, :, 0:64].astype(BF)
    for i, a in enumerate((1, 2, 3)):
        wire.start(xs_.at[lax.rem(xx + a, 4)], xr.at[a - 1], xt[i], 15 + i, 15 + i)
    for i in range(3):
        wire.arrived(xr.at[0], 15 + i)
    for b in range(4):
        acc = keep[0, xx, b]
        ua = upt[xx * 4 + b, :, 0:64]
        for i in range(3):
            acc = acc + xr[i, b, 0:96].astype(F32)
            ua = ua + xr[i, b, 96:144].astype(F32)
        keep[1, 0, b] = acc
        keep[1, 1, b, 0:48] = ua
        ys_[b, 0:96] = acc.astype(BF)
        ys_[b, 96:144] = ua.astype(BF)
    for i, a in enumerate((1, 2, 3)):
        wire.start(ys_.at[lax.rem(y + a, 4)], yr.at[a - 1], yt[i], 18 + i, 18 + i)
    for i in range(3):
        wire.arrived(yr.at[0], 18 + i)
    acc = keep[1, 0, y]
    ua = keep[1, 1, y, 0:48]
    for i in range(3):
        acc = acc + yr[i, 0:96].astype(F32)
        ua = ua + yr[i, 96:144].astype(F32)
    zs[0:96] = acc.astype(BF)
    zs[96:144] = ua.astype(BF)
    for i in range(7):
        wire.start(zs, zr.at[z], zt[i], 21 + i, 21 + i)
    zr[z] = zs[...]
    for i in range(7):
        wire.arrived(zr.at[0], 21 + i)
    scale = 65536**-0.5
    acc = zr[0].astype(F32)
    for i in range(1, 8):
        acc = acc + zr[i].astype(F32)
    acc = acc * scale
    r_out = lax.broadcasted_iota(jnp.int32, (16, 96), 0)
    r_in = lax.broadcasted_iota(jnp.int32, (16, 96), 1)
    pick = jnp.where(z * 12 + r_out == r_in, 1.0, 0.0).astype(F32)
    gd[...] = jnp.dot(
        pick, acc[0:96], preferred_element_type=F32, precision=lax.Precision.HIGHEST
    )
    gu[c, xx, y] = acc[96:144]
    spot = gu.at[c, xx, y]
    for i in range(3):
        wire.start(spot, spot, yt[i], 28 + i, 28 + i)
    for i in range(3):
        wire.arrived(spot, 28 + i)
    for i in range(3):
        wire.start(gu.at[c, xx], gu.at[c, xx], xt[i], 31 + i, 31 + i)
    for i in range(3):
        wire.arrived(gu.at[c, xx], 31 + i)
    wire.start(gu.at[c], gu.at[c], sib, 34, 34)
    wire.arrived(gu.at[c], 34)
    wire.arrived(att.at[:, pl.ds(mine, HALF)], 0)
    keep_att.wait()
    wire.drain()


def reduce(att2, back, upt, x):
    vm = pl.BlockSpec(memory_space=pltpu.VMEM)
    hb = pl.BlockSpec(memory_space=pl.ANY)
    return pl.pallas_call(
        reduce_kernel,
        out_shape=[
            jax.ShapeDtypeStruct((256, 1536), BF),
            jax.ShapeDtypeStruct((16, 64), F32),
            jax.ShapeDtypeStruct((2, 4, 4, 48, 64), F32),
        ],
        in_specs=[hb, vm, vm, vm],
        out_specs=[hb, vm, vm],
        scratch_shapes=[
            pltpu.VMEM((12, 64, 256), BF),
            pltpu.VMEM((12, 64, 256), BF),
            pltpu.VMEM((2, 4, 4, 96, 64), BF),
            pltpu.VMEM((4, 4, 96, 64), BF),
            pltpu.VMEM((2, 4, 4, 96, 64), F32),
            pltpu.VMEM((4, 4, 144, 64), BF),
            pltpu.VMEM((3, 4, 144, 64), BF),
            pltpu.VMEM((4, 144, 64), BF),
            pltpu.VMEM((3, 144, 64), BF),
            pltpu.VMEM((144, 64), BF),
            pltpu.VMEM((8, 144, 64), BF),
            pltpu.SemaphoreType.DMA((35,)),
            pltpu.SemaphoreType.DMA((35,)),
            pltpu.SemaphoreType.DMA((1,)),
        ],
        compiler_params=pltpu.CompilerParams(
            collective_id=2, has_side_effects=True, vmem_limit_bytes=48 * MIB
        ),
        name="reduce",
    )(att2, back, upt, x)


def allowed_row(tile_mask):
    row, col = place()
    r = row + jnp.arange(3, dtype=jnp.int32) - 1
    s = col + jnp.arange(3, dtype=jnp.int32) - 1
    rows = lax.axis_size("row")
    cols = lax.axis_size("col")
    inside = ((r >= 0) & (r < rows))[:, None] & ((s >= 0) & (s < cols))[None, :]
    flags = jnp.where(inside.reshape(9) & (tile_mask.reshape(9) > 0), 1.0, 0.0).astype(F32)
    return jnp.broadcast_to(jnp.repeat(flags, 256)[None], (8, 2304))


def per_device(
    patch_tokens,
    queries,
    key_vectors,
    cotangent,
    value_weight,
    adapter_down,
    adapter_up,
    radius,
    tile_mask,
):
    core = lax.rem(lax.axis_index("row"), 2)
    x = patch_tokens.reshape(256, 3072)
    down = jnp.pad(adapter_down, ((0, 0), (0, 64)))
    low = jnp.dot(x, down, preferred_element_type=F32).astype(BF)
    wp = jnp.pad(value_weight, ((0, 4), (0, 0)))
    q2, kwin, c2, lwin, x2, w, allow2 = gather(
        queries.reshape(256, 1536),
        key_vectors.reshape(256, 1536),
        cotangent.reshape(256, 1536),
        x,
        low,
        wp,
        allowed_row(tile_mask),
    )
    up = lax.dynamic_slice_in_dim(adapter_up, core * HALF, HALF, 1)
    low2 = jnp.concatenate([lwin[4], lwin[7]], axis=0)[:, :64]
    values = (
        jnp.dot(x2.reshape(512, 3072), w.reshape(3072, HALF), preferred_element_type=F32)
        + jnp.dot(low2, up, preferred_element_type=F32)
    ).astype(BF)
    vwin = halo(values.reshape(2, 256, HALF))
    reach = lax.dynamic_slice_in_dim(radius, core * 6, 6, 0).astype(F32)
    att2, back, upt = attention(
        reach, q2, kwin, vwin, c2, lwin, up, jnp.asarray(distances()), allow2
    )
    att, gd, gu = reduce(att2, back, upt.reshape(16, 48, 128), x)
    return att.reshape(16, 16, 1536), gd[:12], gu.reshape(1536, 64).T


def solution(mesh):
    placed = (
        P("row", "col", None),
        P("row", "col", None),
        P("row", "col", None),
        P("row", "col", None),
        P(("row", "col"), None),
        P(),
        P(),
        P(),
        P("row", "col", None),
    )
    return jax.shard_map(
        per_device,
        mesh=mesh,
        in_specs=placed,
        out_specs=(P("row", "col", None), P(("row", "col"), None), P()),
        check_vma=False,
    )
```

time: 1430 us -> 274 us (0.19)
  waiting for transfers between devices: 1100 us -> 0 us
  Pallas kernels: 0 us -> 257 us
  matrix products: 89.5 us -> 9.9 us
  other arithmetic: 63.1 us -> 1.52 us
  starting transfers between devices: 55.3 us -> 0 us
  local copies, waits for them, and re-layouts: 57.6 us -> 4.76 us
  loops' own time: 47 us -> 0 us
    all_gather x1 -> x0, waiting for transfers between devices: 730 us -> none  [per_device(): lax.all_gather(value_weight, ('row', 'col'), axis=0, tiled=True)]
    unnamed x3 -> x0, waiting for transfers between devices: 263 us -> none
    pallas_call x0 -> x4, Pallas kernels: none -> 257 us  [the longest x1 98.3 us: gather(): pl.pallas_call(gather_kernel, out_shape=[jax.ShapeDtypeStruct((2, 256, HA...]
    ppermute x8 -> x0, waiting for transfers between devices: 109 us -> none  [the longest x2 105 us: extended(): after = lax.ppermute(leading, axis, down)]
    dot_general x42 -> x3, matrix products: 89.5 us -> 9.9 us  [the longest x1 5.95 us: per_device(): jnp.dot(x2.reshape(512, 3072), w.reshape(3072, HALF), preferred_element_t...]
    ppermute x8 -> x0, starting transfers between devices: 55.2 us -> none  [the longest x4 40.7 us: shifted(): return lax.ppermute(block, axis, route)]
    another operation x1 -> x0, loops' own time: 47 us -> none  [window_heads(): outputs, grads = lax.map(one_head, jnp.arange(head_count, dtype=jnp.int32))]
    concatenate x3 -> x0, other arithmetic: 25.8 us -> none  [the longest x2 25.7 us: extended(): x = jnp.concatenate([before, x, after], axis=dim)]
  transfers between devices with their start and end apart: 10 -> 0, of which waited for: 7 -> 0; matrix products, arithmetic and copies ran while one was open for 1% -> 0% of each run, Pallas kernels for 0% -> 0%
where the time goes in v1:
time: 274 us
  Pallas kernels  257 us (94%)
  matrix products  9.9 us (4%)
  local copies, waits for them, and re-layouts  4.76 us (2%)
    pallas_call x1, Pallas kernels, gather(): pl.pallas_call(gather_kernel, out_shape=[jax.ShapeDtypeStruct((2, 256, HA...  98.3 us
    pallas_call x1, Pallas kernels, halo(): pl.pallas_call(halo_kernel, out_shape=jax.ShapeDtypeStruct((12, 256, HALF...  61.9 us
    pallas_call x1, Pallas kernels, reduce(): pl.pallas_call(reduce_kernel, out_shape=[jax.ShapeDtypeStruct((256, 1536)...  50.7 us
    pallas_call x1, Pallas kernels, attention(): pl.pallas_call(attention_kernel, grid=(6, 2), out_shape=[jax.ShapeDtypeSt...  46 us
    dot_general x1, matrix products, per_device(): jnp.dot(x2.reshape(512, 3072), w.reshape(3072, HALF), preferred_element_t...  5.95 us

profile of v1, /device:TPU:1, one launch (start us, length us, event | category | flops | bytes accessed | tf_op | source)
XLA Modules:
  0.0 273.9 jit_solution(11260140491239103733)
XLA Ops:
  0.6 0.0 copy-start
  0.7 0.8 dynamic-slice_convert_fusion.radius
  1.4 2.7 fusion.low
  4.2 1.4 pad.9.wp
  5.6 0.1 broadcast_and_fusion
  5.7 0.1 and.42
  5.8 0.7 fusion.3
  6.4 0.1 broadcast_in_dim.22
  6.5 0.6 broadcast_in_dim.24.allow
  7.1 98.3 %gather.1 = (bf16[2,256,768]{2,1,0:T(8,128)(2,1)}, bf16[12,256,768]{2,1,0:T(8,128)(2,1)}, bf16[2,256,768]{2,1,0:T(8,128)(2,1)}, bf16[12,256,128]{2,1,0:T(8,128)(...) custom-call(bf16[256,1536]{1,0:T(8,128)(2,1)} %bitcast.34, ...), custom_call_target="tpu_custom_call" | custom-call | tf_op jit(solution)/shard_map/gather/pallas_call | solution.py:281
  105.4 0.0 copy-start.2
  105.5 5.9 %fusion.6 = f32[512,768]{1,0:T(8,128)S(1)} fusion(bf16[512,3072]{1,0:T(8,128)(2,1)} %bitcast.39, bf16[3072,768]{1,0:T(8,128)(2,1)} %bitcast.38), kind=kOutput, calls=%fused_computation.17 | convolution fusion | flops 2415919104 | bytes 9437184 | tf_op jit(solution)/shard_map/dot_general | solution.py:635
  111.4 0.0 copy-done
  111.4 0.0 copy-done.2
  111.5 1.2 add_convert_fusion
  112.7 0.0 copy-start.3
  112.7 0.0 copy-start.4
  112.7 0.0 copy-start.5
  112.7 61.9 %halo.1.vw = bf16[12,256,768]{2,1,0:T(8,128)(2,1)} custom-call(bf16[2,256,768]{2,1,0:T(8,128)(2,1)} %bitcast.33), custom_call_target="tpu_custom_call" | custom-call | tf_op jit(solution)/shard_map/halo/pallas_call | solution.py:335
  174.6 0.0 copy-done.3
  174.7 0.0 copy-done.4
  174.7 0.0 copy-done.5
  174.7 0.0 copy-start.1
  174.7 46.0 %attention.1 = (bf16[2,256,768]{2,1,0:T(8,128)(2,1)S(1)}, f32[12,64,256]{2,1,0:T(8,128)S(1)}, f32[768,128]{1,0:T(8,128)S(1)}) custom-call(f32[6]{0:T(128)S(1)} %dynamic-slice_convert_fusion.radius, bf16[2,256,768]{2,1,0:T(8,128)(2,1)S(1)} %copy-done.3, bf16[12,256,768]{2,1,0:T(8,128)(2,1)} %get-tuple-element.17.kw, bf16[12,256,768]{2,1,0:T(8,128)(2,1)} %halo.1.vw, ...), custom_call_target="tpu_custom_call" | custom-call | tf_op jit(solution)/shard_map/attention/pallas_call | solution.py:401
  220.7 0.0 copy-done.1
  220.7 50.7 %reduce.1 = (bf16[256,1536]{1,0:T(8,128)(2,1)S(1)}, f32[16,64]{1,0:T(8,128)S(1)}, f32[2,4,4,48,64]{4,3,2,1,0:T(8,128)S(1)}) custom-call(bf16[2,256,768]{2,1,0:T(8,128)(2,1)S(1)} %get-tuple-element.23.att_in, f32[12,64,256]{2,1,0:T(8,128)S(1)} %get-tuple-element.24.back, f32[16,48,128]{2,1,0:T(8,128)S(1)} %bitcast.31, bf16[256,3072]{1,0:T(8,128)(2,1)S(1)} %bitcast.28), custom_call_target="tpu_custom_call" | custom-call | tf_op jit(solution)/shard_map/reduce/pallas_call | solution.py:564
  271.4 1.0 copy.14
  272.4 0.9 copy.18
  273.3 0.6 copy.19
  (4 shorter events, 0.0 us)
Async XLA Ops:
  0.6 110.8 %copy-start = (bf16[64,1536]{1,0:T(8,128)(2,1)S(1)}, bf16[64,1536]{1,0:T(8,128)(2,1)}, u32[]{:S(2)}) copy-start(bf16[64,1536]{1,0:T(8,128)(2,1)} %param.16) | copy-start | bytes 589828
  105.4 6.0 %copy-start.2 = (bf16[12,256,128]{2,1,0:T(8,128)(2,1)S(1)}, bf16[12,256,128]{2,1,0:T(8,128)(2,1)}, u32[]{:S(2)}) copy-start(bf16[12,256,128]{2,1,0:T(8,128)(2,1)} %get-tuple-element.20.low) | copy-start | bytes 2359300
  112.7 61.9 %copy-start.3 = (bf16[2,256,768]{2,1,0:T(8,128)(2,1)S(1)}, bf16[2,256,768]{2,1,0:T(8,128)(2,1)}, u32[]{:S(2)}) copy-start(bf16[2,256,768]{2,1,0:T(8,128)(2,1)} %get-tuple-element.16.q) | copy-start | bytes 2359300
  112.7 62.0 %copy-start.4 = (bf16[2,256,768]{2,1,0:T(8,128)(2,1)S(1)}, bf16[2,256,768]{2,1,0:T(8,128)(2,1)}, u32[]{:S(2)}) copy-start(bf16[2,256,768]{2,1,0:T(8,128)(2,1)} %get-tuple-element.21.cot) | copy-start | bytes 2359300
  112.7 62.0 %copy-start.5 = (f32[2,8,2304]{2,1,0:T(8,128)S(1)}, f32[2,8,2304]{2,1,0:T(8,128)}, u32[]{:S(2)}) copy-start(f32[2,8,2304]{2,1,0:T(8,128)} %get-tuple-element.22.allow) | copy-start | bytes 442372
  174.7 46.0 %copy-start.1 = (bf16[16,16,3072]{2,1,0:T(8,128)(2,1)S(1)}, bf16[16,16,3072]{2,1,0:T(8,128)(2,1)}, u32[]{:S(2)}) copy-start(bf16[16,16,3072]{2,1,0:T(8,128)(2,1)} %param.10) | copy-start | bytes 4718596

commit v2 on v1

v2 whole, which is shorter than its diff:
```python
import jax
import jax.numpy as jnp
import numpy as np
from jax import lax
from jax.experimental import pallas as pl
from jax.experimental.pallas import tpu as pltpu
from jax.sharding import PartitionSpec as P

MESH = pl.DeviceIdType.MESH
BF = jnp.bfloat16
F32 = jnp.float32
HALF = 768
MIB = 2**20


def place():
    row = lax.axis_index("row")
    col = lax.axis_index("col")
    return row, col


def grid_place():
    row, col = place()
    y = lax.div(row, 4)
    x = lax.rem(lax.div(row, 2), 2) * 2 + lax.div(col, 8)
    return y, x, lax.rem(col, 8), lax.rem(row, 2)


def at_grid(y, x, z, c):
    y = lax.rem(y + 4, 4)
    x = lax.rem(x + 4, 4)
    z = lax.rem(z + 8, 8)
    return (y * 4 + lax.div(x, 2) * 2 + c, lax.rem(x, 2) * 8 + z)


def at_chip(k, h, col):
    return (lax.rem(k + 8, 8) * 2 + h, lax.rem(col + 16, 16))


def greet(targets):
    barrier = pltpu.get_barrier_semaphore()
    for target in targets:
        pl.semaphore_signal(barrier, inc=1, device_id=target, device_id_type=MESH)
    pl.semaphore_wait(barrier, len(targets))


class Wire:
    def __init__(self, send, recv):
        self.send, self.recv, self.pending = send, recv, []

    def copy(self, src, dst, target, s, r):
        return pltpu.make_async_remote_copy(
            src_ref=src,
            dst_ref=dst,
            send_sem=self.send.at[s],
            recv_sem=self.recv.at[r],
            device_id=target,
            device_id_type=MESH,
        )

    def start(self, src, dst, target, s, r):
        copy = self.copy(src, dst, target, s, r)
        copy.start()
        self.pending.append(copy)

    def arrived(self, dst, r):
        row, col = place()
        self.copy(dst, dst, (row + 1 - 2 * lax.rem(row, 2), col), r, r).wait_recv()

    def drain(self):
        for copy in self.pending:
            copy.wait_send()
        self.pending = []


def chip_targets():
    row, col = place()
    k, c = lax.div(row, 2), lax.rem(row, 2)
    out = [at_chip(k, 1 - c, col)]
    for h in (0, 1):
        out += [at_chip(k + 1, h, col), at_chip(k - 1, h, col)]
        out += [at_chip(k, h, col + 1), at_chip(k, h, col - 1)]
    return out


def stretch(c):
    return pl.multiple_of(c * HALF, HALF)


def kernel(
    radius, q, kv, cot, x, wp, allow, down, up, dist,
    att, gd, gu,
    q2, kwin, c2, lwin, x2, wout, allow2, zbuf, wblk, low,
    vwin, s_ref, p_ref, back, upt, att2,
    bs, br, gs, gr, keep, xs_, xr, ys_, yr, zs, zr,
    send, recv, local,
):
    row, col = place()
    k, c = lax.div(row, 2), lax.rem(row, 2)
    y, xx, z, _ = grid_place()
    other = 1 - c
    mine = stretch(c)
    wire = Wire(send, recv)
    targets = chip_targets()
    for a in range(1, 8):
        targets += [at_grid(y, xx, z + a, 0), at_grid(y, xx, z + a, 1)]
    xt = [at_grid(y, xx + a, z, c) for a in (1, 2, 3)]
    yt = [at_grid(y + a, xx, z, c) for a in (1, 2, 3)]
    zt = [at_grid(y, xx, z + a, c) for a in range(1, 8)]
    targets += xt + yt
    for h in (0, 1):
        for d in (1, -1):
            targets += [at_chip(k + 1, h, col + d), at_chip(k - 1, h, col + d)]
    sib = at_chip(k, other, col)
    theirs = stretch(other)

    locals_ = []

    def local_copy(src, dst):
        copy = pltpu.make_async_copy(src, dst, local.at[len(locals_)])
        copy.start()
        locals_.append(copy)
        return copy

    slot = c * 8 + z
    centre = (1 + c) * 3 + 1
    own_x = local_copy(x, x2.at[c])
    own_w = local_copy(wp.at[:, pl.ds(mine, HALF)], zbuf.at[slot])
    local_copy(kv.at[:, pl.ds(mine, HALF)], kwin.at[centre])
    local_copy(q.at[:, pl.ds(mine, HALF)], q2.at[c])
    local_copy(cot.at[:, pl.ds(mine, HALF)], c2.at[c])
    local_copy(allow, allow2.at[c])
    greet(targets)

    wire.start(wp.at[:, pl.ds(theirs, HALF)], zbuf.at[slot], sib, 0, 0)
    for a in range(1, 8):
        for h in (0, 1):
            hh = c if h == 0 else other
            wire.start(
                wp.at[:, pl.ds(stretch(hh), HALF)],
                zbuf.at[slot],
                at_grid(y, xx, z + a, hh),
                2 * a + h,
                2 * a + h,
            )
    far = (3 - 3 * c) * 3 + 1
    step = 2 * c - 1

    def spread_tile(src, win, n, split):
        part = lambda h: src.at[:, pl.ds(h * HALF, HALF)] if split else src
        for h in (0, 1):
            wire.start(part(h), win.at[far], at_chip(k + step, h, col), n + h, n + c)
        for h in (0, 1):
            for i, d in enumerate((1, -1)):
                m = n + 2 + 2 * i
                spot = win.at[(1 + c) * 3 + 1 - d]
                wire.start(part(h), spot, at_chip(k, h, col + d), m + h, m + c)
        full = src.at[:, pl.ds(theirs, HALF)] if split else src
        wire.start(full, win.at[centre], sib, n + 6, n + 6)

    spread_tile(kv, kwin, 16, True)
    wire.start(q.at[:, pl.ds(theirs, HALF)], q2.at[c], sib, 30, 30)
    wire.start(cot.at[:, pl.ds(theirs, HALF)], c2.at[c], sib, 31, 31)
    wire.start(x, x2.at[c], sib, 32, 32)
    wire.start(allow, allow2.at[c], sib, 33, 33)
    own_x.wait()
    low[...] = jnp.dot(x2[c], down[...], preferred_element_type=F32).astype(BF)
    lwin[centre] = low[...]
    spread_tile(low, lwin, 23, False)

    own_w.wait()
    wire.arrived(zbuf.at[0], 0)
    for a in range(1, 8):
        for h in (0, 1):
            wire.arrived(zbuf.at[0], 2 * a + h)
    r_out = lax.broadcasted_iota(jnp.int32, (96, 128), 0)
    r_in = lax.broadcasted_iota(jnp.int32, (96, 128), 1)
    pick = jnp.where(lax.div(r_out, 12) * 16 + lax.rem(r_out, 12) == r_in, 1.0, 0.0).astype(BF)
    for cc in (0, 1):
        part = zbuf[pl.ds(cc * 8, 8)].reshape(128, HALF)
        wblk[cc] = jnp.dot(pick, part, preferred_element_type=F32).astype(BF)

    xs = (at_grid(y, xx + 1, z, c), at_grid(y, xx - 1, z, c))
    ys = (at_grid(y + 1, xx, z, c), at_grid(y - 1, xx, z, c))

    def x_part(i):
        i = lax.rem(i + 4, 4)
        return lax.div(i, 2), lax.rem(i, 2)

    def y_part(i):
        return lax.rem(i + 4, 4)

    def small(yi, xi):
        a, b = x_part(xi)
        return wout.at[y_part(yi), a, :, b]

    def small_half(yi, xi, j):
        a, b = x_part(xi)
        return wout.at[y_part(yi), a, j, b]

    def strip(xi):
        a, b = x_part(xi)
        return wout.at[:, a, :, b]

    def strip_half(xi, j):
        a, b = x_part(xi)
        return wout.at[:, a, j, b]

    own_copy = pltpu.make_async_copy(wblk, small(y, xx), local.at[7])
    own_copy.start()

    def corners(wire, win, n, m):
        for rr, first in ((0, n + 1), (3, n)):
            wire.arrived(win.at[rr * 3 + 1], first)
            for d in (1, -1):
                spot = win.at[rr * 3 + 1 - d]
                wire.start(win.at[rr * 3 + 1], spot, at_chip(k, c, col + d), m, m)
                m += 1

    def ring(wire, index, block, half, n, targets, src):
        nxt, prv = targets
        wire.start(src, block(index), nxt, n, n)
        wire.start(src, block(index), prv, n + 1, n + 1)

        def second():
            wire.arrived(block(index), n)
            wire.start(half(index - 1, 0), half(index - 1, 0), nxt, n + 2, n + 2)
            wire.arrived(block(index), n + 1)
            wire.start(half(index + 1, 1), half(index + 1, 1), prv, n + 3, n + 3)

        def last():
            wire.arrived(half(index, 0), n + 2)
            wire.arrived(half(index, 1), n + 3)

        return second, last

    def spread(along_x):
        sub = Wire(send, recv)
        x_small = (xx, lambda i: small(y, i), lambda i, j: small_half(y, i, j))
        y_small = (y, lambda i: small(i, xx), lambda i, j: small_half(i, xx, j))
        x_big = (xx, strip, strip_half)
        y_big = (y, lambda i: wout.at[y_part(i)], lambda i, j: wout.at[y_part(i), j])
        one, two = (x_small, y_big) if along_x else (y_small, x_big)
        first_to, second_to = (xs, ys) if along_x else (ys, xs)
        second, last = ring(sub, *one, 34, first_to, wblk)
        second()
        corners(sub, kwin, 16, 42)
        corners(sub, lwin, 23, 46)
        last()
        own_copy.wait()
        second, last = ring(sub, *two, 38, second_to, two[1](two[0]))
        second()
        last()
        sub.drain()

    @pl.when(c == 0)
    def _():
        spread(True)

    @pl.when(c == 1)
    def _():
        spread(False)

    wire.arrived(x2.at[0], 32)
    wire.arrived(lwin.at[0], 29)
    low2 = jnp.concatenate([lwin[4][:, :64], lwin[7][:, :64]], axis=0)

    @pl.loop(0, 3)
    def _(n):
        lanes = pl.ds(pl.multiple_of(n * 256, 256), 256)
        acc = jnp.dot(low2, up[:, lanes], preferred_element_type=F32)
        for yi in range(4):
            rows = wout[yi, :, :, :, :, lanes].reshape(768, 256)
            part = x2[:, :, yi * 768 : (yi + 1) * 768].reshape(512, 768)
            acc = acc + jnp.dot(part, rows, preferred_element_type=F32)
        acc = acc.astype(BF)
        vwin[4, :, lanes] = acc[:256]
        vwin[7, :, lanes] = acc[256:]

    v0 = 50
    sides = [at_chip(k, c, col + d) for d in (1, -1)]
    wire.start(vwin.at[4], vwin.at[10], at_chip(k - 1, c, col), v0, v0)
    wire.start(vwin.at[7], vwin.at[1], at_chip(k + 1, c, col), v0 + 1, v0 + 1)
    for i, d in enumerate((1, -1)):
        for t in (0, 1):
            m = v0 + 2 + 2 * i + t
            wire.start(vwin.at[4 + 3 * t], vwin.at[(1 + t) * 3 + 1 - d], sides[i], m, m)

    for cc in (0, 1):
        for i in (0, 1):
            wire.arrived(kwin.at[0], 18 + 2 * i + cc)
            wire.arrived(lwin.at[0], 25 + 2 * i + cc)
    wire.arrived(kwin.at[0], 22)
    wire.arrived(q2.at[0], 30)
    wire.arrived(c2.at[0], 31)
    wire.arrived(allow2.at[0], 33)
    for n in range(4):
        wire.arrived(kwin.at[0], 42 + n)
        wire.arrived(lwin.at[0], 46 + n)
    for copy in locals_[2:]:
        copy.wait()

    back[...] = jnp.zeros_like(back)
    upt[...] = jnp.zeros_like(upt)

    def probs(lo, hi):
        @pl.loop(lo, hi)
        def _(i):
            h, t = lax.div(i, 2), lax.rem(i, 2)
            lanes = pl.ds(pl.multiple_of(h * 128, 128), 128)
            keys = kwin[pl.ds(t * 3, 9), :, lanes].reshape(2304, 128)
            s_ref[...] = lax.dot_general(
                q2[t, :, lanes], keys, (((1,), (1,)), ((), ())), preferred_element_type=F32
            )
            limit = allow2[t, 0:1, :] * (radius[h] * radius[h] + 1.0) - 1.0

            @pl.loop(0, 8)
            def _(j):
                rows = pl.ds(pl.multiple_of(j * 32, 32), 32)
                s = jnp.where(dist[rows] <= limit, s_ref[rows] * 128**-0.5, -1e30)
                e = jnp.exp(s - jnp.max(s, axis=1, keepdims=True))
                p_ref[i, rows] = (e * (1.0 / jnp.sum(e, axis=1, keepdims=True))).astype(BF)

            vgt = jnp.dot(c2[t, :, lanes].T, p_ref[i], preferred_element_type=F32).astype(BF)
            bt = jnp.dot(up[:, lanes], vgt, preferred_element_type=F32)
            for n in range(9):
                back[t * 3 + n] += bt[:, n * 256 : (n + 1) * 256]
            lows = lwin[pl.ds(t * 3, 9)].reshape(2304, 128)
            rows = pl.ds(pl.multiple_of(h * 128, 128), 128)
            upt[rows] += jnp.dot(vgt, lows, preferred_element_type=F32)

    def attend(lo, hi):
        @pl.loop(lo, hi)
        def _(i):
            h, t = lax.div(i, 2), lax.rem(i, 2)
            lanes = pl.ds(pl.multiple_of(h * 128, 128), 128)
            vals = vwin[pl.ds(t * 3, 9), :, lanes].reshape(2304, 128)
            att2[t, :, lanes] = jnp.dot(p_ref[i], vals, preferred_element_type=F32).astype(BF)

    probs(0, 6)
    n = v0 + 6
    for rr in (3, 0):
        wire.arrived(vwin.at[rr * 3 + 1], v0 if rr else v0 + 1)
        for i, d in enumerate((1, -1)):
            wire.start(vwin.at[rr * 3 + 1], vwin.at[rr * 3 + 1 - d], sides[i], n, n)
            n += 1
    probs(6, 12)

    def values_here():
        for n in range(2, 10):
            wire.arrived(vwin.at[0], v0 + n)

    r0 = 60
    around = [(rr, cc) for rr in range(4) for cc in range(3)]
    for n, (rr, cc) in enumerate(around):
        bs[n] = back[n].astype(BF)
    for n, (rr, cc) in enumerate(around):
        dk, h = ((-1, 1), (0, 0), (0, 1), (1, 0))[rr]
        adj = 0 if rr in (1, 2) else 1
        slot = adj * 6 + cc * 2
        if (rr, cc) in ((1, 1), (2, 1)):
            @pl.when(c != h)
            def _():
                copy = wire.copy(bs.at[n], br.at[slot + c], sib, r0 + 1, r0 + 2 + slot + c)
                copy.start()
                copy.wait_send()
        else:
            wire.start(
                bs.at[n], br.at[slot + c], at_chip(k + dk, h, col + cc - 1), r0 + 2 + n, r0 + 2 + slot + c
            )
    total = back[(1 + c) * 3 + 1]
    wire.arrived(br.at[0], r0 + 4 + other)
    total = total + br[2 + other].astype(F32)
    for slot in range(12):
        if slot not in (2, 3):
            wire.arrived(br.at[0], r0 + 2 + slot)
            total = total + br[slot].astype(F32)
    hi = total.astype(BF)
    lo = (total - hi.astype(F32)).astype(BF)
    both = jnp.concatenate([hi, lo], axis=0)

    @pl.loop(0, 8)
    def _(i):
        part = x2[c, :, pl.ds(pl.multiple_of(i * 384, 384), 384)]
        g = jnp.dot(both, part, preferred_element_type=F32)
        g = (g[:64] + g[64:]).T
        yi, xhi = lax.div(i, 2), lax.rem(i, 2)
        for cc in (0, 1):
            for xl in (0, 1):
                rows = g[(cc * 2 + xl) * 96 : (cc * 2 + xl + 1) * 96]
                keep[cc, xhi * 2 + xl, yi] = rows
                gs[cc, xhi * 2 + xl, yi] = rows.astype(BF)

    wire.start(gs.at[other], gr, sib, r0 + 14, r0 + 14)
    wire.arrived(gr, r0 + 14)
    for a in range(4):
        for b in range(4):
            full = keep[c, a, b] + gr[a, b].astype(F32)
            keep[0, a, b] = full
            xs_[a, b, 0:96] = full.astype(BF)
            xs_[a, b, 96:144] = upt[(a * 4 + b) * 48 : (a * 4 + b + 1) * 48, 0:64].astype(BF)
    for i, a in enumerate((1, 2, 3)):
        wire.start(xs_.at[lax.rem(xx + a, 4)], xr.at[a - 1], xt[i], r0 + 15 + i, r0 + 15 + i)
    for i in range(3):
        wire.arrived(xr.at[0], r0 + 15 + i)
    for b in range(4):
        acc = keep[0, xx, b]
        ua = upt[pl.ds(pl.multiple_of((xx * 4 + b) * 48, 16), 48), 0:64]
        for i in range(3):
            acc = acc + xr[i, b, 0:96].astype(F32)
            ua = ua + xr[i, b, 96:144].astype(F32)
        keep[1, 0, b] = acc
        keep[1, 1, b, 0:48] = ua
        ys_[b, 0:96] = acc.astype(BF)
        ys_[b, 96:144] = ua.astype(BF)
    for i, a in enumerate((1, 2, 3)):
        wire.start(ys_.at[lax.rem(y + a, 4)], yr.at[a - 1], yt[i], r0 + 18 + i, r0 + 18 + i)
    for i in range(3):
        wire.arrived(yr.at[0], r0 + 18 + i)
    acc = keep[1, 0, y]
    ua = keep[1, 1, y, 0:48]
    for i in range(3):
        acc = acc + yr[i, 0:96].astype(F32)
        ua = ua + yr[i, 96:144].astype(F32)
    zs[0:96] = acc.astype(BF)
    zs[96:144] = ua.astype(BF)
    for i in range(7):
        wire.start(zs, zr.at[z], zt[i], r0 + 21 + i, r0 + 21 + i)
    zr[z] = zs[...]
    for i in range(7):
        wire.arrived(zr.at[0], r0 + 21 + i)
    scale = 65536**-0.5
    acc = zr[0].astype(F32)
    for i in range(1, 8):
        acc = acc + zr[i].astype(F32)
    acc = acc * scale
    r_out = lax.broadcasted_iota(jnp.int32, (16, 96), 0)
    r_in = lax.broadcasted_iota(jnp.int32, (16, 96), 1)
    pick = jnp.where(z * 12 + r_out == r_in, 1.0, 0.0).astype(F32)
    gd[...] = jnp.dot(
        pick, acc[0:96], preferred_element_type=F32, precision=lax.Precision.HIGHEST
    )
    gu[c, xx, y] = acc[96:144]
    spot = gu.at[c, xx, y]
    for i in range(3):
        wire.start(spot, spot, yt[i], r0 + 28 + i, r0 + 28 + i)
    for i in range(3):
        wire.arrived(spot, r0 + 28 + i)
    for i in range(3):
        wire.start(gu.at[c, xx], gu.at[c, xx], xt[i], r0 + 31 + i, r0 + 31 + i)
    for i in range(3):
        wire.arrived(gu.at[c, xx], r0 + 31 + i)
    wire.start(gu.at[c], gu.at[c], sib, r0 + 34, r0 + 34)
    wire.arrived(gu.at[c], r0 + 34)
    values_here()
    attend(0, 12)
    wire.start(att2.at[other], att.at[:, pl.ds(mine, HALF)], sib, r0, r0)
    keep_att = pltpu.make_async_copy(att2.at[c], att.at[:, pl.ds(mine, HALF)], local.at[6])
    keep_att.start()
    wire.arrived(att.at[:, pl.ds(mine, HALF)], r0)
    keep_att.wait()
    wire.drain()


def distances():
    qp = np.arange(256)
    kp = np.arange(2304)
    kr = (kp // 768) * 16 + (kp % 256) // 16 - 16
    kc = (kp // 256 % 3) * 16 + kp % 16 - 16
    dr = kr[None] - (qp // 16)[:, None]
    dc = kc[None] - (qp % 16)[:, None]
    return (dr * dr + dc * dc).astype(np.float32)


def fused(*args):
    vm = pl.BlockSpec(memory_space=pltpu.VMEM)
    hb = pl.BlockSpec(memory_space=pl.ANY)
    return pl.pallas_call(
        kernel,
        out_shape=[
            jax.ShapeDtypeStruct((256, 1536), BF),
            jax.ShapeDtypeStruct((16, 64), F32),
            jax.ShapeDtypeStruct((2, 4, 4, 48, 64), F32),
        ],
        in_specs=[pl.BlockSpec(memory_space=pltpu.SMEM), hb, hb, hb, hb, hb, hb, vm, vm, vm],
        out_specs=[hb, vm, vm],
        scratch_shapes=[
            pltpu.VMEM((2, 256, HALF), BF),
            pltpu.VMEM((12, 256, HALF), BF),
            pltpu.VMEM((2, 256, HALF), BF),
            pltpu.VMEM((12, 256, 128), BF),
            pltpu.VMEM((2, 256, 3072), BF),
            pltpu.VMEM((4, 2, 2, 2, 96, HALF), BF),
            pltpu.VMEM((2, 8, 2304), F32),
            pltpu.VMEM((16, 16, HALF), BF),
            pltpu.VMEM((2, 96, HALF), BF),
            pltpu.VMEM((256, 128), BF),
            pltpu.VMEM((12, 256, HALF), BF),
            pltpu.VMEM((256, 2304), F32),
            pltpu.VMEM((12, 256, 2304), BF),
            pltpu.VMEM((12, 64, 256), F32),
            pltpu.VMEM((HALF, 128), F32),
            pltpu.VMEM((2, 256, HALF), BF),
            pltpu.VMEM((12, 64, 256), BF),
            pltpu.VMEM((12, 64, 256), BF),
            pltpu.VMEM((2, 4, 4, 96, 64), BF),
            pltpu.VMEM((4, 4, 96, 64), BF),
            pltpu.VMEM((2, 4, 4, 96, 64), F32),
            pltpu.VMEM((4, 4, 144, 64), BF),
            pltpu.VMEM((3, 4, 144, 64), BF),
            pltpu.VMEM((4, 144, 64), BF),
            pltpu.VMEM((3, 144, 64), BF),
            pltpu.VMEM((144, 64), BF),
            pltpu.VMEM((8, 144, 64), BF),
            pltpu.SemaphoreType.DMA((96,)),
            pltpu.SemaphoreType.DMA((96,)),
            pltpu.SemaphoreType.DMA((8,)),
        ],
        compiler_params=pltpu.CompilerParams(
            collective_id=0, has_side_effects=True, vmem_limit_bytes=60 * MIB
        ),
        name="fused",
    )(*args)


def allowed_row(tile_mask):
    row, col = place()
    r = row + jnp.arange(3, dtype=jnp.int32) - 1
    s = col + jnp.arange(3, dtype=jnp.int32) - 1
    rows = lax.axis_size("row")
    cols = lax.axis_size("col")
    inside = ((r >= 0) & (r < rows))[:, None] & ((s >= 0) & (s < cols))[None, :]
    flags = jnp.where(inside.reshape(9) & (tile_mask.reshape(9) > 0), 1.0, 0.0).astype(F32)
    return jnp.broadcast_to(jnp.repeat(flags, 256)[None], (8, 2304))


def per_device(
    patch_tokens,
    queries,
    key_vectors,
    cotangent,
    value_weight,
    adapter_down,
    adapter_up,
    radius,
    tile_mask,
):
    core = lax.rem(lax.axis_index("row"), 2)
    att, gd, gu = fused(
        lax.dynamic_slice_in_dim(radius, core * 6, 6, 0).astype(F32),
        queries.reshape(256, 1536),
        key_vectors.reshape(256, 1536),
        cotangent.reshape(256, 1536),
        patch_tokens.reshape(256, 3072),
        jnp.pad(value_weight, ((0, 4), (0, 0))),
        allowed_row(tile_mask),
        jnp.pad(adapter_down, ((0, 0), (0, 64))),
        lax.dynamic_slice_in_dim(adapter_up, core * HALF, HALF, 1),
        jnp.asarray(distances()),
    )
    return att.reshape(16, 16, 1536), gd[:12], gu.reshape(1536, 64).T


def solution(mesh):
    placed = (
        P("row", "col", None),
        P("row", "col", None),
        P("row", "col", None),
        P("row", "col", None),
        P(("row", "col"), None),
        P(),
        P(),
        P(),
        P("row", "col", None),
    )
    return jax.shard_map(
        per_device,
        mesh=mesh,
        in_specs=placed,
        out_specs=(P("row", "col", None), P(("row", "col"), None), P()),
        check_vma=False,
    )
```

time: 274 us -> 239 us (0.87)
  Pallas kernels: 257 us -> 226 us
  matrix products: 9.9 us -> 0 us
  local copies, waits for them, and re-layouts: 4.76 us -> 10.1 us
    pallas_call x4 -> x1, Pallas kernels: 257 us -> 226 us  [fused(): pl.pallas_call(kernel, out_shape=[jax.ShapeDtypeStruct((256, 1536), BF),...]
    dot_general x3 -> x0, matrix products: 9.9 us -> none  [the longest x1 5.95 us: per_device(): jnp.dot(x2.reshape(512, 3072), w.reshape(3072, HALF), preferred_element_t...]
where the time goes in v2:
time: 239 us
  Pallas kernels  226 us (95%)
  local copies, waits for them, and re-layouts  10.1 us (4%)
    pallas_call x1, Pallas kernels, fused(): pl.pallas_call(kernel, out_shape=[jax.ShapeDtypeStruct((256, 1536), BF),...  226 us

profile of v2, /device:TPU:1, one launch (start us, length us, event | category | flops | bytes accessed | tf_op | source)
XLA Modules:
  0.0 238.7 jit_solution(755190461482128063)
XLA Ops:
  0.6 0.0 copy-start
  0.7 1.3 dynamic-slice_convert_fusion.radius
  2.0 0.1 broadcast_and_fusion
  2.0 0.1 and.42
  2.1 0.7 fusion
  2.8 0.1 broadcast_in_dim.22
  2.9 1.4 pad.8.wp
  4.3 0.6 broadcast_in_dim.24.allow
  4.9 0.0 copy-done
  4.9 0.6 constant_dynamic-slice_fusion.up
  5.6 1.4 copy.13
  6.9 1.0 pad.9.down
  8.0 225.9 %fused.1 = (bf16[256,1536]{1,0:T(8,128)(2,1)}, f32[16,64]{1,0:T(8,128)}, f32[2,4,4,48,64]{4,3,2,1,0:T(8,128)}) custom-call(f32[6]{0:T(128)} %dynamic-slice_convert_fusion.radius, bf16[256,1536]{1,0:T(8,128)(2,1)} %bitcast.15, bf16[256,1536]{1,0:T(8,128)(2,1)} %bitcast.16, bf16[256,1536]{1,0:T(8,128)(2,1)} %bitcast.17, bf16[256,3072]{1,0:T(8,128)(2,1)} %bitcast.12, ...), custom_call_target="tpu_custom_call" | custom-call | tf_op jit(solution)/shard_map/fused/pallas_call | solution.py:478
  233.9 0.0 copy-start.1
  233.9 2.1 copy.14
  236.0 2.1 copy.17
  238.1 0.0 copy-done.1
  238.1 0.6 copy.18
  (2 shorter events, 0.0 us)
Async XLA Ops:
  0.6 4.3 %copy-start = (bf16[64,1536]{1,0:T(8,128)(2,1)S(1)}, bf16[64,1536]{1,0:T(8,128)(2,1)}, u32[]{:S(2)}) copy-start(bf16[64,1536]{1,0:T(8,128)(2,1)} %param.16) | copy-start | bytes 589828
  233.9 4.2 %copy-start.1 = (f32[16,64]{1,0:T(8,128)S(1)}, f32[16,64]{1,0:T(8,128)}, u32[]{:S(2)}) copy-start(f32[16,64]{1,0:T(8,128)} %get-tuple-element.7) | copy-start | bytes 12292

commit v3 on v2

--- a/solution.py
+++ b/solution.py
@@ -92,7 +92,7 @@
     att, gd, gu,
     q2, kwin, c2, lwin, x2, wout, allow2, zbuf, wblk, low,
     vwin, s_ref, p_ref, back, upt, att2,
-    bs, br, gs, gr, keep, xs_, xr, ys_, yr, zs, zr,
+    bs, br, gs, gr, keep, ux, uxr, ukeep, uy, uyr, uz, uzr, gx, gxr, gy, gyr, gz, gzr,
     send, recv, local,
 ):
     row, col = place()
@@ -108,6 +108,7 @@
     yt = [at_grid(y + a, xx, z, c) for a in (1, 2, 3)]
     zt = [at_grid(y, xx, z + a, c) for a in range(1, 8)]
     targets += xt + yt
+    targets += [(row, lax.rem(col + d, 16)) for d in (7, 8, 9)]
     for h in (0, 1):
         for d in (1, -1):
             targets += [at_chip(k + 1, h, col + d), at_chip(k - 1, h, col + d)]
@@ -146,18 +147,93 @@
     far = (3 - 3 * c) * 3 + 1
     step = 2 * c - 1
 
+    def inner(d):
+        return col != (15 if d == 1 else 0)
+
+    def side_sends(parts, win, rr, n, m):
+        for h, target_core, src in parts:
+            for i, d in enumerate((1, -1)):
+
+                @pl.when(inner(d))
+                def _(h=h, i=i, d=d, src=src, target_core=target_core):
+                    wire.copy(
+                        src,
+                        win.at[rr * 3 + 1 - d],
+                        at_chip(k, target_core, col + d),
+                        n + 2 * i + h,
+                        m[i],
+                    ).start()
+
+    def side_drain(src, n, count):
+        for h in range(count):
+            for i, d in enumerate((1, -1)):
+
+                @pl.when(inner(d))
+                def _(h=h, i=i):
+                    wire.copy(src, src, sib, n + 2 * i + h, n + 2 * i + h).wait_send()
+
+    def side_arrivals(win, n):
+        for i, d in enumerate((1, -1)):
+
+            @pl.when(inner(-d))
+            def _(i=i):
+                wire.arrived(win.at[0], n + 2 * i)
+                wire.arrived(win.at[0], n + 2 * i + 1)
+
+    def clear_edges(win):
+        for edge, cc in ((0, 0), (15, 2)):
+
+            @pl.when(col == edge)
+            def _(cc=cc):
+                for rr in (1, 2):
+                    win[rr * 3 + cc] = jnp.zeros(win.shape[1:], win.dtype)
+
+    def corner(win, m, rr):
+        base = m + (2 if rr else 0)
+        src = win.at[rr * 3 + 1]
+        for i, (d, hop, relay) in enumerate(((1, 7, 15), (-1, 8, 0))):
+            spot, near = win.at[rr * 3 + 1 - d], win.at[rr * 3 + 1 + d]
+
+            @pl.when((col != hop) & (col != relay))
+            def _(d=d, i=i, spot=spot):
+                wire.copy(src, spot, at_chip(k, c, col + d), base + i, base + i).start()
+
+            @pl.when(col == hop)
+            def _(i=i, near=near, relay=relay):
+                wire.copy(src, near, (row, jnp.int32(relay)), base + i, base + 1 - i).start()
+
+    def corner_relay(win, m, rr):
+        base = m + (2 if rr else 0)
+        for i, (d, hop, relay) in enumerate(((1, 7, 15), (-1, 8, 0))):
+            spot, near = win.at[rr * 3 + 1 - d], win.at[rr * 3 + 1 + d]
+
+            @pl.when(col == relay)
+            def _(i=i, d=d, spot=spot, near=near, hop=hop):
+                wire.arrived(near, base + 1 - i)
+                wire.copy(near, spot, (row, jnp.int32(hop + d)), base + i, base + i).start()
+
+    def corner_arrivals(win, m):
+        for rr in (0, 3):
+            base = m + (2 if rr else 0)
+            for i, relay in enumerate((0, 15)):
+
+                @pl.when(col != relay)
+                def _(i=i):
+                    wire.arrived(win.at[0], base + i)
+        for n in range(4):
+            wire.copy(win.at[0], win.at[0], sib, m + n, m + n).wait_send()
+
     def spread_tile(src, win, n, split):
         part = lambda h: src.at[:, pl.ds(h * HALF, HALF)] if split else src
         for h in (0, 1):
             wire.start(part(h), win.at[far], at_chip(k + step, h, col), n + h, n + c)
-        for h in (0, 1):
-            for i, d in enumerate((1, -1)):
-                m = n + 2 + 2 * i
-                spot = win.at[(1 + c) * 3 + 1 - d]
-                wire.start(part(h), spot, at_chip(k, h, col + d), m + h, m + c)
+        parts = [(h, h, part(h)) for h in (0, 1)]
+        side_sends(parts, win, 1 + c, n + 2, (n + 2 + c, n + 4 + c))
         full = src.at[:, pl.ds(theirs, HALF)] if split else src
         wire.start(full, win.at[centre], sib, n + 6, n + 6)
 
+    for win in (kwin, lwin, vwin):
+        clear_edges(win)
     spread_tile(kv, kwin, 16, True)
     wire.start(q.at[:, pl.ds(theirs, HALF)], q2.at[c], sib, 30, 30)
     wire.start(cot.at[:, pl.ds(theirs, HALF)], c2.at[c], sib, 31, 31)
@@ -198,59 +274,60 @@
         a, b = x_part(xi)
         return wout.at[y_part(yi), a, j, b]
 
-    def strip(xi):
-        a, b = x_part(xi)
-        return wout.at[:, a, :, b]
-
-    def strip_half(xi, j):
-        a, b = x_part(xi)
-        return wout.at[:, a, j, b]
-
     own_copy = pltpu.make_async_copy(wblk, small(y, xx), local.at[7])
     own_copy.start()
 
-    def corners(wire, win, n, m):
+    def corners(win, n, m):
         for rr, first in ((0, n + 1), (3, n)):
             wire.arrived(win.at[rr * 3 + 1], first)
-            for d in (1, -1):
-                spot = win.at[rr * 3 + 1 - d]
-                wire.start(win.at[rr * 3 + 1], spot, at_chip(k, c, col + d), m, m)
-                m += 1
-
-    def ring(wire, index, block, half, n, targets, src):
-        nxt, prv = targets
-        wire.start(src, block(index), nxt, n, n)
-        wire.start(src, block(index), prv, n + 1, n + 1)
-
-        def second():
-            wire.arrived(block(index), n)
-            wire.start(half(index - 1, 0), half(index - 1, 0), nxt, n + 2, n + 2)
-            wire.arrived(block(index), n + 1)
-            wire.start(half(index + 1, 1), half(index + 1, 1), prv, n + 3, n + 3)
-
-        def last():
-            wire.arrived(half(index, 0), n + 2)
-            wire.arrived(half(index, 1), n + 3)
-
-        return second, last
+            corner(win, m, rr)
 
     def spread(along_x):
         sub = Wire(send, recv)
-        x_small = (xx, lambda i: small(y, i), lambda i, j: small_half(y, i, j))
-        y_small = (y, lambda i: small(i, xx), lambda i, j: small_half(i, xx, j))
-        x_big = (xx, strip, strip_half)
-        y_big = (y, lambda i: wout.at[y_part(i)], lambda i, j: wout.at[y_part(i), j])
-        one, two = (x_small, y_big) if along_x else (y_small, x_big)
-        first_to, second_to = (xs, ys) if along_x else (ys, xs)
-        second, last = ring(sub, *one, 34, first_to, wblk)
-        second()
-        corners(sub, kwin, 16, 42)
-        corners(sub, lwin, 23, 46)
-        last()
+        w0 = 34
+        if along_x:
+            one, two = xs, ys
+            full = lambda a, b: small(y + b, xx + a)
+            half = lambda a, b, j: small_half(y + b, xx + a, j)
+        else:
+            one, two = ys, xs
+            full = lambda a, b: small(y + a, xx + b)
+            half = lambda a, b, j: small_half(y + a, xx + b, j)
+        at = (0, -1, 1, 2)
+
+        def across(n, src):
+            for i in (0, 1):
+                sub.start(src, full(at[n], 0), two[i], w0 + 4 + 2 * n + i, w0 + 4 + 2 * n + i)
+
+        def pass_on(n):
+            for i, d in enumerate((-1, 1)):
+                sub.arrived(full(at[n], d), w0 + 4 + 2 * n + i)
+                m = w0 + 12 + 2 * n + i
+                sub.start(half(at[n], d, i), half(at[n], d, i), two[i], m, m)
+
+        for i in (0, 1):
+            sub.start(wblk, full(0, 0), one[i], w0 + i, w0 + i)
+        across(0, wblk)
+        for i, d in enumerate((-1, 1)):
+            sub.arrived(full(d, 0), w0 + i)
+            sub.start(half(d, 0, i), half(d, 0, i), one[i], w0 + 2 + i, w0 + 2 + i)
+            across(1 + i, full(d, 0))
+        corners(kwin, 16, 70)
+        pass_on(0)
+        for i in (0, 1):
+            sub.arrived(half(2, 0, i), w0 + 2 + i)
+        across(3, full(2, 0))
+        corners(lwin, 23, 74)
+        pass_on(1)
+        pass_on(2)
+        for win, m in ((kwin, 70), (lwin, 74)):
+            for rr in (0, 3):
+                corner_relay(win, m, rr)
+        pass_on(3)
+        for n in range(4):
+            for i in (0, 1):
+                sub.arrived(half(0, 2, i), w0 + 12 + 2 * n + i)
         own_copy.wait()
-        second, last = ring(sub, *two, 38, second_to, two[1](two[0]))
-        second()
-        last()
         sub.drain()
 
     @pl.when(c == 0)
@@ -277,26 +354,23 @@
         vwin[4, :, lanes] = acc[:256]
         vwin[7, :, lanes] = acc[256:]
 
-    v0 = 50
-    sides = [at_chip(k, c, col + d) for d in (1, -1)]
+    v0 = 54
     wire.start(vwin.at[4], vwin.at[10], at_chip(k - 1, c, col), v0, v0)
     wire.start(vwin.at[7], vwin.at[1], at_chip(k + 1, c, col), v0 + 1, v0 + 1)
-    for i, d in enumerate((1, -1)):
-        for t in (0, 1):
-            m = v0 + 2 + 2 * i + t
-            wire.start(vwin.at[4 + 3 * t], vwin.at[(1 + t) * 3 + 1 - d], sides[i], m, m)
-
-    for cc in (0, 1):
-        for i in (0, 1):
-            wire.arrived(kwin.at[0], 18 + 2 * i + cc)
-            wire.arrived(lwin.at[0], 25 + 2 * i + cc)
+    for t in (0, 1):
+        m = v0 + 2 + t
+        side_sends([(t, c, vwin.at[4 + 3 * t])], vwin, 1 + t, v0 + 2, (m, m + 2))
+
+    side_arrivals(kwin, 18)
+    side_arrivals(lwin, 25)
     wire.arrived(kwin.at[0], 22)
     wire.arrived(q2.at[0], 30)
     wire.arrived(c2.at[0], 31)
     wire.arrived(allow2.at[0], 33)
-    for n in range(4):
-        wire.arrived(kwin.at[0], 42 + n)
-        wire.arrived(lwin.at[0], 46 + n)
+    corner_arrivals(kwin, 70)
+    corner_arrivals(lwin, 74)
+    side_drain(kwin.at[0], 18, 2)
+    side_drain(lwin.at[0], 25, 2)
     for copy in locals_[2:]:
         copy.wait()
 
@@ -337,47 +411,64 @@
             vals = vwin[pl.ds(t * 3, 9), :, lanes].reshape(2304, 128)
             att2[t, :, lanes] = jnp.dot(p_ref[i], vals, preferred_element_type=F32).astype(BF)
 
-    probs(0, 6)
-    n = v0 + 6
-    for rr in (3, 0):
-        wire.arrived(vwin.at[rr * 3 + 1], v0 if rr else v0 + 1)
-        for i, d in enumerate((1, -1)):
-            wire.start(vwin.at[rr * 3 + 1], vwin.at[rr * 3 + 1 - d], sides[i], n, n)
-            n += 1
-    probs(6, 12)
+    probs(0, 5)
+    wire.arrived(vwin.at[10], v0)
+    corner(vwin, 60, 3)
+    wire.arrived(vwin.at[1], v0 + 1)
+    corner(vwin, 60, 0)
+    probs(5, 8)
+    corner_relay(vwin, 60, 3)
+    corner_relay(vwin, 60, 0)
+    probs(8, 12)
 
     def values_here():
-        for n in range(2, 10):
-            wire.arrived(vwin.at[0], v0 + n)
-
-    r0 = 60
-    around = [(rr, cc) for rr in range(4) for cc in range(3)]
-    for n, (rr, cc) in enumerate(around):
+        side_arrivals(vwin, v0 + 2)
+        corner_arrivals(vwin, 60)
+        side_drain(vwin.at[0], v0 + 2, 2)
+
+    b0 = 78
+    for n in range(12):
+        rr, cc = n // 3, n % 3
         bs[n] = back[n].astype(BF)
-    for n, (rr, cc) in enumerate(around):
         dk, h = ((-1, 1), (0, 0), (0, 1), (1, 0))[rr]
-        adj = 0 if rr in (1, 2) else 1
-        slot = adj * 6 + cc * 2
-        if (rr, cc) in ((1, 1), (2, 1)):
+        slot = (0 if rr in (1, 2) else 6) + cc * 2
+        if n in (4, 7):
+
             @pl.when(c != h)
             def _():
-                copy = wire.copy(bs.at[n], br.at[slot + c], sib, r0 + 1, r0 + 2 + slot + c)
-                copy.start()
-                copy.wait_send()
+                wire.copy(bs.at[n], br.at[slot + c], sib, b0 + 12, b0 + slot + c).start()
         else:
-            wire.start(
-                bs.at[n], br.at[slot + c], at_chip(k + dk, h, col + cc - 1), r0 + 2 + n, r0 + 2 + slot + c
-            )
+            target = at_chip(k + dk, h, col + cc - 1)
+            wire.start(bs.at[n], br.at[slot + c], target, b0 + n, b0 + slot + c)
+
+    u0, e0 = 92, 116
+    for a in range(4):
+        for b in range(4):
+            ux[a, b] = upt[(a * 4 + b) * 48 : (a * 4 + b + 1) * 48, 0:64].astype(BF)
+    for i in range(3):
+        wire.start(ux.at[lax.rem(xx + i + 1, 4)], uxr.at[i], xt[i], u0 + i, u0 + i)
+
     total = back[(1 + c) * 3 + 1]
-    wire.arrived(br.at[0], r0 + 4 + other)
+    wire.arrived(br.at[0], b0 + 2 + other)
     total = total + br[2 + other].astype(F32)
     for slot in range(12):
         if slot not in (2, 3):
-            wire.arrived(br.at[0], r0 + 2 + slot)
+            wire.arrived(br.at[0], b0 + slot)
             total = total + br[slot].astype(F32)
     hi = total.astype(BF)
     lo = (total - hi.astype(F32)).astype(BF)
     both = jnp.concatenate([hi, lo], axis=0)
+
+    for i in range(3):
+        wire.arrived(uxr.at[0], u0 + i)
+    for b in range(4):
+        ua = upt[pl.ds(pl.multiple_of((xx * 4 + b) * 48, 16), 48), 0:64]
+        for i in range(3):
+            ua = ua + uxr[i, b].astype(F32)
+        ukeep[b] = ua
+        uy[b] = ua.astype(BF)
+    for i in range(3):
+        wire.start(uy.at[lax.rem(y + i + 1, 4)], uyr.at[i], yt[i], u0 + 3 + i, u0 + 3 + i)
 
     @pl.loop(0, 8)
     def _(i):
@@ -391,74 +482,91 @@
                 keep[cc, xhi * 2 + xl, yi] = rows
                 gs[cc, xhi * 2 + xl, yi] = rows.astype(BF)
 
-    wire.start(gs.at[other], gr, sib, r0 + 14, r0 + 14)
-    wire.arrived(gr, r0 + 14)
+    wire.start(gs.at[other], gr, sib, e0, e0)
+
+    for i in range(3):
+        wire.arrived(uyr.at[0], u0 + 3 + i)
+    ua = ukeep[y]
+    for i in range(3):
+        ua = ua + uyr[i].astype(F32)
+    uz[...] = ua.astype(BF)
+    uzr[z] = ua.astype(BF)
+    for i in range(7):
+        wire.start(uz, uzr.at[z], zt[i], u0 + 6 + i, u0 + 6 + i)
+
+    wire.arrived(gr, e0)
     for a in range(4):
         for b in range(4):
             full = keep[c, a, b] + gr[a, b].astype(F32)
             keep[0, a, b] = full
-            xs_[a, b, 0:96] = full.astype(BF)
-            xs_[a, b, 96:144] = upt[(a * 4 + b) * 48 : (a * 4 + b + 1) * 48, 0:64].astype(BF)
-    for i, a in enumerate((1, 2, 3)):
-        wire.start(xs_.at[lax.rem(xx + a, 4)], xr.at[a - 1], xt[i], r0 + 15 + i, r0 + 15 + i)
-    for i in range(3):
-        wire.arrived(xr.at[0], r0 + 15 + i)
+            gx[a, b] = full.astype(BF)
+    for i in range(3):
+        wire.start(gx.at[lax.rem(xx + i + 1, 4)], gxr.at[i], xt[i], e0 + 1 + i, e0 + 1 + i)
+
+    scale = 65536**-0.5
+    for i in range(7):
+        wire.arrived(uz, u0 + 6 + i)
+    ua = uzr[0].astype(F32)
+    for i in range(1, 8):
+        ua = ua + uzr[i].astype(F32)
+    gu[c, xx, y] = ua * scale
+    spot = gu.at[c, xx, y]
+    for i in range(3):
+        wire.start(spot, spot, yt[i], u0 + 13 + i, u0 + 13 + i)
+
+    for i in range(3):
+        wire.arrived(gxr.at[0], e0 + 1 + i)
     for b in range(4):
         acc = keep[0, xx, b]
-        ua = upt[pl.ds(pl.multiple_of((xx * 4 + b) * 48, 16), 48), 0:64]
         for i in range(3):
-            acc = acc + xr[i, b, 0:96].astype(F32)
-            ua = ua + xr[i, b, 96:144].astype(F32)
+            acc = acc + gxr[i, b].astype(F32)
         keep[1, 0, b] = acc
-        keep[1, 1, b, 0:48] = ua
-        ys_[b, 0:96] = acc.astype(BF)
-        ys_[b, 96:144] = ua.astype(BF)
-    for i, a in enumerate((1, 2, 3)):
-        wire.start(ys_.at[lax.rem(y + a, 4)], yr.at[a - 1], yt[i], r0 + 18 + i, r0 + 18 + i)
-    for i in range(3):
-        wire.arrived(yr.at[0], r0 + 18 + i)
+        gy[b] = acc.astype(BF)
+    for i in range(3):
+        wire.start(gy.at[lax.rem(y + i + 1, 4)], gyr.at[i], yt[i], e0 + 4 + i, e0 + 4 + i)
+
+    for i in range(3):
+        wire.arrived(spot, u0 + 13 + i)
+    for i in range(3):
+        wire.start(gu.at[c, xx], gu.at[c, xx], xt[i], u0 + 16 + i, u0 + 16 + i)
+
+    values_here()
+    attend(0, 6)
+
+    for i in range(3):
+        wire.arrived(gyr.at[0], e0 + 4 + i)
     acc = keep[1, 0, y]
-    ua = keep[1, 1, y, 0:48]
-    for i in range(3):
-        acc = acc + yr[i, 0:96].astype(F32)
-        ua = ua + yr[i, 96:144].astype(F32)
-    zs[0:96] = acc.astype(BF)
-    zs[96:144] = ua.astype(BF)
+    for i in range(3):
+        acc = acc + gyr[i].astype(F32)
+    r_out = lax.broadcasted_iota(jnp.int32, (128, 96), 0)
+    r_in = lax.broadcasted_iota(jnp.int32, (128, 96), 1)
+    row_of = lax.div(r_out, 16) * 12 + lax.rem(r_out, 16)
+    pick = jnp.where((row_of == r_in) & (lax.rem(r_out, 16) < 12), 1.0, 0.0).astype(BF)
+    parts = jnp.dot(pick, acc.astype(BF), preferred_element_type=F32).astype(BF)
+    for i in range(8):
+        gz[i] = parts[i * 16 : (i + 1) * 16]
     for i in range(7):
-        wire.start(zs, zr.at[z], zt[i], r0 + 21 + i, r0 + 21 + i)
-    zr[z] = zs[...]
-    for i in range(7):
-        wire.arrived(zr.at[0], r0 + 21 + i)
-    scale = 65536**-0.5
-    acc = zr[0].astype(F32)
-    for i in range(1, 8):
-        acc = acc + zr[i].astype(F32)
-    acc = acc * scale
-    r_out = lax.broadcasted_iota(jnp.int32, (16, 96), 0)
-    r_in = lax.broadcasted_iota(jnp.int32, (16, 96), 1)
-    pick = jnp.where(z * 12 + r_out == r_in, 1.0, 0.0).astype(F32)
-    gd[...] = jnp.dot(
-        pick, acc[0:96], preferred_element_type=F32, precision=lax.Precision.HIGHEST
-    )
-    gu[c, xx, y] = acc[96:144]
-    spot = gu.at[c, xx, y]
-    for i in range(3):
-        wire.start(spot, spot, yt[i], r0 + 28 + i, r0 + 28 + i)
-    for i in range(3):
-        wire.arrived(spot, r0 + 28 + i)
-    for i in range(3):
-        wire.start(gu.at[c, xx], gu.at[c, xx], xt[i], r0 + 31 + i, r0 + 31 + i)
-    for i in range(3):
-        wire.arrived(gu.at[c, xx], r0 + 31 + i)
-    wire.start(gu.at[c], gu.at[c], sib, r0 + 34, r0 + 34)
-    wire.arrived(gu.at[c], r0 + 34)
-    values_here()
-    attend(0, 12)
-    wire.start(att2.at[other], att.at[:, pl.ds(mine, HALF)], sib, r0, r0)
+        wire.start(gz.at[lax.rem(z + i + 1, 8)], gzr.at[i], zt[i], e0 + 7 + i, e0 + 7 + i)
+
+    for i in range(3):
+        wire.arrived(gu.at[c, xx], u0 + 16 + i)
+    wire.start(gu.at[c], gu.at[c], sib, u0 + 19, u0 + 19)
+
+    attend(6, 12)
+    wire.start(att2.at[other], att.at[:, pl.ds(mine, HALF)], sib, e0 + 14, e0 + 14)
     keep_att = pltpu.make_async_copy(att2.at[c], att.at[:, pl.ds(mine, HALF)], local.at[6])
     keep_att.start()
-    wire.arrived(att.at[:, pl.ds(mine, HALF)], r0)
+
+    for i in range(7):
+        wire.arrived(gzr.at[0], e0 + 7 + i)
+    acc = gz[z].astype(F32)
+    for i in range(7):
+        acc = acc + gzr[i].astype(F32)
+    gd[...] = acc * scale
+    wire.arrived(gu.at[c], u0 + 19)
+    wire.arrived(att.at[:, pl.ds(mine, HALF)], e0 + 14)
     keep_att.wait()
+    wire.copy(bs.at[0], bs.at[0], sib, b0 + 12, b0 + 12).wait_send()
     wire.drain()
 
 
@@ -506,14 +614,21 @@
             pltpu.VMEM((2, 4, 4, 96, 64), BF),
             pltpu.VMEM((4, 4, 96, 64), BF),
             pltpu.VMEM((2, 4, 4, 96, 64), F32),
-            pltpu.VMEM((4, 4, 144, 64), BF),
-            pltpu.VMEM((3, 4, 144, 64), BF),
-            pltpu.VMEM((4, 144, 64), BF),
-            pltpu.VMEM((3, 144, 64), BF),
-            pltpu.VMEM((144, 64), BF),
-            pltpu.VMEM((8, 144, 64), BF),
-            pltpu.SemaphoreType.DMA((96,)),
-            pltpu.SemaphoreType.DMA((96,)),
+            pltpu.VMEM((4, 4, 48, 64), BF),
+            pltpu.VMEM((3, 4, 48, 64), BF),
+            pltpu.VMEM((4, 48, 64), F32),
+            pltpu.VMEM((4, 48, 64), BF),
+            pltpu.VMEM((3, 48, 64), BF),
+            pltpu.VMEM((48, 64), BF),
+            pltpu.VMEM((8, 48, 64), BF),
+            pltpu.VMEM((4, 4, 96, 64), BF),
+            pltpu.VMEM((3, 4, 96, 64), BF),
+            pltpu.VMEM((4, 96, 64), BF),
+            pltpu.VMEM((3, 96, 64), BF),
+            pltpu.VMEM((8, 16, 64), BF),
+            pltpu.VMEM((7, 16, 64), BF),
+            pltpu.SemaphoreType.DMA((136,)),
+            pltpu.SemaphoreType.DMA((136,)),
             pltpu.SemaphoreType.DMA((8,)),
         ],
         compiler_params=pltpu.CompilerParams(

time: 239 us -> 190 us (0.79)
  Pallas kernels: 226 us -> 177 us
    pallas_call x1, Pallas kernels: 226 us -> 177 us  [fused(): pl.pallas_call(kernel, out_shape=[jax.ShapeDtypeStruct((256, 1536), BF),...]
where the time goes in v3:
time: 190 us
  Pallas kernels  177 us (93%)
  local copies, waits for them, and re-layouts  10.1 us (5%)
  other arithmetic  2.03 us (1%)
    pallas_call x1, Pallas kernels, fused(): pl.pallas_call(kernel, out_shape=[jax.ShapeDtypeStruct((256, 1536), BF),...  177 us
    unnamed x7, local copies, waits for them, and re-layouts  4.04 us

profile of v3, /device:TPU:1, one launch (start us, length us, event | category | flops | bytes accessed | tf_op | source)
XLA Modules:
  0.0 190.1 jit_solution(818860079128934877)
XLA Ops:
  0.6 0.0 copy-start
  0.7 1.3 dynamic-slice_convert_fusion.radius
  2.0 0.1 broadcast_and_fusion
  2.0 0.1 and.42
  2.1 0.7 fusion
  2.8 0.1 broadcast_in_dim.22
  2.9 1.4 pad.8.wp
  4.3 0.6 broadcast_in_dim.24.allow
  4.9 0.0 copy-done
  4.9 0.6 constant_dynamic-slice_fusion.up
  5.6 1.4 copy.13
  6.9 1.0 pad.9.down
  8.0 177.3 %fused.1 = (bf16[256,1536]{1,0:T(8,128)(2,1)}, f32[16,64]{1,0:T(8,128)}, f32[2,4,4,48,64]{4,3,2,1,0:T(8,128)}) custom-call(f32[6]{0:T(128)} %dynamic-slice_convert_fusion.radius, bf16[256,1536]{1,0:T(8,128)(2,1)} %bitcast.15, bf16[256,1536]{1,0:T(8,128)(2,1)} %bitcast.16, bf16[256,1536]{1,0:T(8,128)(2,1)} %bitcast.17, bf16[256,3072]{1,0:T(8,128)(2,1)} %bitcast.12, ...), custom_call_target="tpu_custom_call" | custom-call | tf_op jit(solution)/shard_map/fused/pallas_call | solution.py:586
  185.3 0.0 copy-start.1
  185.3 2.1 %copy.14 = f32[1536,64]{0,1:T(8,128)} copy(f32[1536,64]{1,0:T(8,128)} %bitcast.14) | data formatting | bytes 786432 | tf_op jit(solution)/shard_map/reshape | solution.py:676
  187.5 2.1 %copy.17 = bf16[16,16,1536]{2,1,0:T(8,128)(2,1)} copy(bf16[16,16,1536]{2,1,0:T(8,128)(2,1)} %bitcast.13) | data formatting | bytes 1572864
  189.5 0.0 copy-done.1
  189.5 0.6 copy.18
  (2 shorter events, 0.0 us)
Async XLA Ops:
  0.6 4.3 %copy-start = (bf16[64,1536]{1,0:T(8,128)(2,1)S(1)}, bf16[64,1536]{1,0:T(8,128)(2,1)}, u32[]{:S(2)}) copy-start(bf16[64,1536]{1,0:T(8,128)(2,1)} %param.16) | copy-start | bytes 589828
  185.3 4.2 %copy-start.1 = (f32[16,64]{1,0:T(8,128)S(1)}, f32[16,64]{1,0:T(8,128)}, u32[]{:S(2)}) copy-start(f32[16,64]{1,0:T(8,128)} %get-tuple-element.7) | copy-start | bytes 12292

commit v4 on v3

--- a/solution.py
+++ b/solution.py
@@ -88,9 +88,9 @@
 
 
 def kernel(
-    radius, q, kv, cot, x, wp, allow, down, up, dist,
+    radius, mask, q, kv, cot, x, w, down, up, dist,
     att, gd, gu,
-    q2, kwin, c2, lwin, x2, wout, allow2, zbuf, wblk, low,
+    q2, kwin, c2, lwin, x2, wout, allow2, zbuf, wblk, low, wp, gun,
     vwin, s_ref, p_ref, back, upt, att2,
     bs, br, gs, gr, keep, ux, uxr, ukeep, uy, uyr, uz, uzr, gx, gxr, gy, gyr, gz, gzr,
     send, recv, local,
@@ -108,7 +108,7 @@
     yt = [at_grid(y + a, xx, z, c) for a in (1, 2, 3)]
     zt = [at_grid(y, xx, z + a, c) for a in range(1, 8)]
     targets += xt + yt
-    targets += [(row, lax.rem(col + d, 16)) for d in (7, 8, 9)]
+    targets += [at_chip(k, h, col + d) for d in (7, 8, 9) for h in (0, 1)]
     for h in (0, 1):
         for d in (1, -1):
             targets += [at_chip(k + 1, h, col + d), at_chip(k - 1, h, col + d)]
@@ -126,11 +126,19 @@
     slot = c * 8 + z
     centre = (1 + c) * 3 + 1
     own_x = local_copy(x, x2.at[c])
-    own_w = local_copy(wp.at[:, pl.ds(mine, HALF)], zbuf.at[slot])
     local_copy(kv.at[:, pl.ds(mine, HALF)], kwin.at[centre])
     local_copy(q.at[:, pl.ds(mine, HALF)], q2.at[c])
     local_copy(cot.at[:, pl.ds(mine, HALF)], c2.at[c])
-    local_copy(allow, allow2.at[c])
+    for n in range(9):
+        r, t = row + n // 3 - 1, col + n % 3 - 1
+        seen = (r >= 0) & (r < 16) & (t >= 0) & (t < 16) & (mask[0, 0, n] > 0)
+        allow2[c, :, n * 256 : (n + 1) * 256] = jnp.full((8, 256), jnp.where(seen, 1.0, 0.0))
+    r_out = lax.broadcasted_iota(jnp.int32, (16, 12), 0)
+    r_in = lax.broadcasted_iota(jnp.int32, (16, 12), 1)
+    wp[...] = jnp.dot(
+        jnp.where(r_out == r_in, 1.0, 0.0).astype(BF), w[...], preferred_element_type=F32
+    ).astype(BF)
+    local_copy(wp.at[:, pl.ds(mine, HALF)], zbuf.at[slot])
     greet(targets)
 
     wire.start(wp.at[:, pl.ds(theirs, HALF)], zbuf.at[slot], sib, 0, 0)
@@ -147,88 +155,79 @@
     far = (3 - 3 * c) * 3 + 1
     step = 2 * c - 1
 
-    def inner(d):
-        return col != (15 if d == 1 else 0)
-
-    def side_sends(parts, win, rr, n, m):
+    crossing = ((0, 1, 7, 15), (1, -1, 8, 0))
+
+    def side_sends(parts, win, rr, n, which):
         for h, target_core, src in parts:
-            for i, d in enumerate((1, -1)):
-
-                @pl.when(inner(d))
-                def _(h=h, i=i, d=d, src=src, target_core=target_core):
-                    wire.copy(
-                        src,
-                        win.at[rr * 3 + 1 - d],
-                        at_chip(k, target_core, col + d),
-                        n + 2 * i + h,
-                        m[i],
-                    ).start()
-
-    def side_drain(src, n, count):
-        for h in range(count):
-            for i, d in enumerate((1, -1)):
-
-                @pl.when(inner(d))
-                def _(h=h, i=i):
-                    wire.copy(src, src, sib, n + 2 * i + h, n + 2 * i + h).wait_send()
+            for i, d, hop, relay in crossing:
+                spot, near = win.at[rr * 3 + 1 - d], win.at[rr * 3 + 1 + d]
+
+                @pl.when((col != hop) & (col != relay))
+                def _(h=h, i=i, d=d, src=src, target_core=target_core, spot=spot):
+                    target = at_chip(k, target_core, col + d)
+                    wire.copy(src, spot, target, n + 2 * i + h, n + 2 * i + which).start()
+
+                @pl.when(col == hop)
+                def _(h=h, i=i, src=src, target_core=target_core, near=near, relay=relay):
+                    target = at_chip(k, target_core, jnp.int32(relay))
+                    wire.copy(src, near, target, n + 2 * i + h, n + 2 * (1 - i) + which).start()
+
+    def side_relay(win, n):
+        for i, d, hop, relay in crossing:
+
+            @pl.when(col == relay)
+            def _(i=i, d=d, hop=hop):
+                for t in (0, 1):
+                    spot, near = win.at[(1 + t) * 3 + 1 - d], win.at[(1 + t) * 3 + 1 + d]
+                    wire.arrived(near, n + 2 * (1 - i) + t)
+                    m = n + 2 * i + t
+                    wire.copy(near, spot, (row, jnp.int32(hop + d)), m, m).start()
 
     def side_arrivals(win, n):
-        for i, d in enumerate((1, -1)):
-
-            @pl.when(inner(-d))
+        for i, edge in enumerate((0, 15)):
+
+            @pl.when(col != edge)
             def _(i=i):
                 wire.arrived(win.at[0], n + 2 * i)
                 wire.arrived(win.at[0], n + 2 * i + 1)
 
+        for m in range(4):
+            wire.copy(win.at[0], win.at[0], sib, n + m, n + m).wait_send()
+
     def clear_edges(win):
         for edge, cc in ((0, 0), (15, 2)):
 
             @pl.when(col == edge)
             def _(cc=cc):
-                for rr in (1, 2):
+                for rr in (0, 3):
                     win[rr * 3 + cc] = jnp.zeros(win.shape[1:], win.dtype)
 
     def corner(win, m, rr):
-        base = m + (2 if rr else 0)
         src = win.at[rr * 3 + 1]
-        for i, (d, hop, relay) in enumerate(((1, 7, 15), (-1, 8, 0))):
-            spot, near = win.at[rr * 3 + 1 - d], win.at[rr * 3 + 1 + d]
-
-            @pl.when((col != hop) & (col != relay))
-            def _(d=d, i=i, spot=spot):
-                wire.copy(src, spot, at_chip(k, c, col + d), base + i, base + i).start()
-
-            @pl.when(col == hop)
-            def _(i=i, near=near, relay=relay):
-                wire.copy(src, near, (row, jnp.int32(relay)), base + i, base + 1 - i).start()
-
-    def corner_relay(win, m, rr):
-        base = m + (2 if rr else 0)
-        for i, (d, hop, relay) in enumerate(((1, 7, 15), (-1, 8, 0))):
-            spot, near = win.at[rr * 3 + 1 - d], win.at[rr * 3 + 1 + d]
-
-            @pl.when(col == relay)
-            def _(i=i, d=d, spot=spot, near=near, hop=hop):
-                wire.arrived(near, base + 1 - i)
-                wire.copy(near, spot, (row, jnp.int32(hop + d)), base + i, base + i).start()
+        for i, d, _, edge in crossing:
+
+            @pl.when(col != edge)
+            def _(i=i, d=d):
+                n = m + (2 if rr else 0) + i
+                wire.copy(src, win.at[rr * 3 + 1 - d], at_chip(k, c, col + d), n, n).start()
 
     def corner_arrivals(win, m):
-        for rr in (0, 3):
-            base = m + (2 if rr else 0)
-            for i, relay in enumerate((0, 15)):
-
-                @pl.when(col != relay)
-                def _(i=i):
-                    wire.arrived(win.at[0], base + i)
-        for n in range(4):
-            wire.copy(win.at[0], win.at[0], sib, m + n, m + n).wait_send()
+        for n in (m, m + 2):
+            for i, edge in enumerate((0, 15)):
+
+                @pl.when(col != edge)
+                def _(n=n, i=i):
+                    wire.arrived(win.at[0], n + i)
+
+                @pl.when(col != 15 - edge)
+                def _(n=n, i=i):
+                    wire.copy(win.at[0], win.at[0], sib, n + i, n + i).wait_send()
 
     def spread_tile(src, win, n, split):
         part = lambda h: src.at[:, pl.ds(h * HALF, HALF)] if split else src
         for h in (0, 1):
             wire.start(part(h), win.at[far], at_chip(k + step, h, col), n + h, n + c)
-        parts = [(h, h, part(h)) for h in (0, 1)]
-        side_sends(parts, win, 1 + c, n + 2, (n + 2 + c, n + 4 + c))
+        side_sends([(h, h, part(h)) for h in (0, 1)], win, 1 + c, n + 2, c)
         full = src.at[:, pl.ds(theirs, HALF)] if split else src
         wire.start(full, win.at[centre], sib, n + 6, n + 6)
 
@@ -238,13 +237,16 @@
     wire.start(q.at[:, pl.ds(theirs, HALF)], q2.at[c], sib, 30, 30)
     wire.start(cot.at[:, pl.ds(theirs, HALF)], c2.at[c], sib, 31, 31)
     wire.start(x, x2.at[c], sib, 32, 32)
-    wire.start(allow, allow2.at[c], sib, 33, 33)
+    wire.start(allow2.at[c], allow2.at[c], sib, 33, 33)
     own_x.wait()
-    low[...] = jnp.dot(x2[c], down[...], preferred_element_type=F32).astype(BF)
+    low[:, 0:64] = lax.dot_general(
+        x2[c], down[...], (((1,), (1,)), ((), ())), preferred_element_type=F32
+    ).astype(BF)
+    low[:, 64:128] = jnp.zeros((256, 64), BF)
     lwin[centre] = low[...]
     spread_tile(low, lwin, 23, False)
 
-    own_w.wait()
+    locals_.pop().wait()
     wire.arrived(zbuf.at[0], 0)
     for a in range(1, 8):
         for h in (0, 1):
@@ -313,16 +315,15 @@
             sub.start(half(d, 0, i), half(d, 0, i), one[i], w0 + 2 + i, w0 + 2 + i)
             across(1 + i, full(d, 0))
         corners(kwin, 16, 70)
+        side_relay(kwin, 18)
         pass_on(0)
         for i in (0, 1):
             sub.arrived(half(2, 0, i), w0 + 2 + i)
         across(3, full(2, 0))
         corners(lwin, 23, 74)
+        side_relay(lwin, 25)
         pass_on(1)
         pass_on(2)
-        for win, m in ((kwin, 70), (lwin, 74)):
-            for rr in (0, 3):
-                corner_relay(win, m, rr)
         pass_on(3)
         for n in range(4):
             for i in (0, 1):
@@ -330,13 +331,18 @@
         own_copy.wait()
         sub.drain()
 
-    @pl.when(c == 0)
+    busy = lax.rem(z + 1, 8) < 2
+
+    @pl.when((c == 0) | busy)
     def _():
         spread(True)
 
-    @pl.when(c == 1)
+    @pl.when((c == 1) & jnp.logical_not(busy))
     def _():
         spread(False)
+
+    def heads(start, width):
+        return pl.ds(pl.multiple_of(mine + start, 128), width)
 
     wire.arrived(x2.at[0], 32)
     wire.arrived(lwin.at[0], 29)
@@ -345,7 +351,7 @@
     @pl.loop(0, 3)
     def _(n):
         lanes = pl.ds(pl.multiple_of(n * 256, 256), 256)
-        acc = jnp.dot(low2, up[:, lanes], preferred_element_type=F32)
+        acc = jnp.dot(low2, up[:, heads(n * 256, 256)], preferred_element_type=F32)
         for yi in range(4):
             rows = wout[yi, :, :, :, :, lanes].reshape(768, 256)
             part = x2[:, :, yi * 768 : (yi + 1) * 768].reshape(512, 768)
@@ -358,8 +364,7 @@
     wire.start(vwin.at[4], vwin.at[10], at_chip(k - 1, c, col), v0, v0)
     wire.start(vwin.at[7], vwin.at[1], at_chip(k + 1, c, col), v0 + 1, v0 + 1)
     for t in (0, 1):
-        m = v0 + 2 + t
-        side_sends([(t, c, vwin.at[4 + 3 * t])], vwin, 1 + t, v0 + 2, (m, m + 2))
+        side_sends([(t, c, vwin.at[4 + 3 * t])], vwin, 1 + t, v0 + 2, t)
 
     side_arrivals(kwin, 18)
     side_arrivals(lwin, 25)
@@ -369,9 +374,7 @@
     wire.arrived(allow2.at[0], 33)
     corner_arrivals(kwin, 70)
     corner_arrivals(lwin, 74)
-    side_drain(kwin.at[0], 18, 2)
-    side_drain(lwin.at[0], 25, 2)
-    for copy in locals_[2:]:
+    for copy in locals_[1:]:
         copy.wait()
 
     back[...] = jnp.zeros_like(back)
@@ -386,7 +389,8 @@
             s_ref[...] = lax.dot_general(
                 q2[t, :, lanes], keys, (((1,), (1,)), ((), ())), preferred_element_type=F32
             )
-            limit = allow2[t, 0:1, :] * (radius[h] * radius[h] + 1.0) - 1.0
+            reach = radius[c * 6 + h]
+            limit = allow2[t, 0:1, :] * (reach * reach + 1).astype(F32) - 1.0
 
             @pl.loop(0, 8)
             def _(j):
@@ -396,7 +400,7 @@
                 p_ref[i, rows] = (e * (1.0 / jnp.sum(e, axis=1, keepdims=True))).astype(BF)
 
             vgt = jnp.dot(c2[t, :, lanes].T, p_ref[i], preferred_element_type=F32).astype(BF)
-            bt = jnp.dot(up[:, lanes], vgt, preferred_element_type=F32)
+            bt = jnp.dot(up[:, heads(h * 128, 128)], vgt, preferred_element_type=F32)
             for n in range(9):
                 back[t * 3 + n] += bt[:, n * 256 : (n + 1) * 256]
             lows = lwin[pl.ds(t * 3, 9)].reshape(2304, 128)
@@ -416,15 +420,12 @@
     corner(vwin, 60, 3)
     wire.arrived(vwin.at[1], v0 + 1)
     corner(vwin, 60, 0)
-    probs(5, 8)
-    corner_relay(vwin, 60, 3)
-    corner_relay(vwin, 60, 0)
-    probs(8, 12)
+    side_relay(vwin, v0 + 2)
+    probs(5, 12)
 
     def values_here():
         side_arrivals(vwin, v0 + 2)
         corner_arrivals(vwin, 60)
-        side_drain(vwin.at[0], v0 + 2, 2)
 
     b0 = 78
     for n in range(12):
@@ -509,8 +510,8 @@
     ua = uzr[0].astype(F32)
     for i in range(1, 8):
         ua = ua + uzr[i].astype(F32)
-    gu[c, xx, y] = ua * scale
-    spot = gu.at[c, xx, y]
+    gun[c, xx, y] = ua * scale
+    spot = gun.at[c, xx, y]
     for i in range(3):
         wire.start(spot, spot, yt[i], u0 + 13 + i, u0 + 13 + i)
 
@@ -528,7 +529,7 @@
     for i in range(3):
         wire.arrived(spot, u0 + 13 + i)
     for i in range(3):
-        wire.start(gu.at[c, xx], gu.at[c, xx], xt[i], u0 + 16 + i, u0 + 16 + i)
+        wire.start(gun.at[c, xx], gun.at[c, xx], xt[i], u0 + 16 + i, u0 + 16 + i)
 
     values_here()
     attend(0, 6)
@@ -549,8 +550,8 @@
         wire.start(gz.at[lax.rem(z + i + 1, 8)], gzr.at[i], zt[i], e0 + 7 + i, e0 + 7 + i)
 
     for i in range(3):
-        wire.arrived(gu.at[c, xx], u0 + 16 + i)
-    wire.start(gu.at[c], gu.at[c], sib, u0 + 19, u0 + 19)
+        wire.arrived(gun.at[c, xx], u0 + 16 + i)
+    wire.start(gun.at[c], gun.at[c], sib, u0 + 19, u0 + 19)
 
     attend(6, 12)
     wire.start(att2.at[other], att.at[:, pl.ds(mine, HALF)], sib, e0 + 14, e0 + 14)
@@ -562,8 +563,12 @@
     acc = gz[z].astype(F32)
     for i in range(7):
         acc = acc + gzr[i].astype(F32)
-    gd[...] = acc * scale
-    wire.arrived(gu.at[c], u0 + 19)
+    gd[...] = (acc * scale)[0:12]
+    wire.arrived(gun.at[c], u0 + 19)
+    for cc in (0, 1):
+        for i in (0, 2):
+            lanes = pl.ds(cc * HALF + i * 192, 384)
+            gu[:, lanes] = gun[cc, i : i + 2].reshape(384, 64).T
     wire.arrived(att.at[:, pl.ds(mine, HALF)], e0 + 14)
     keep_att.wait()
     wire.copy(bs.at[0], bs.at[0], sib, b0 + 12, b0 + 12).wait_send()
@@ -587,10 +592,10 @@
         kernel,
         out_shape=[
             jax.ShapeDtypeStruct((256, 1536), BF),
-            jax.ShapeDtypeStruct((16, 64), F32),
-            jax.ShapeDtypeStruct((2, 4, 4, 48, 64), F32),
+            jax.ShapeDtypeStruct((12, 64), F32),
+            jax.ShapeDtypeStruct((64, 1536), F32),
         ],
-        in_specs=[pl.BlockSpec(memory_space=pltpu.SMEM), hb, hb, hb, hb, hb, hb, vm, vm, vm],
+        in_specs=[pl.BlockSpec(memory_space=pltpu.SMEM)] * 2 + [hb] * 4 + [vm] * 4,
         out_specs=[hb, vm, vm],
         scratch_shapes=[
             pltpu.VMEM((2, 256, HALF), BF),
@@ -603,6 +608,8 @@
             pltpu.VMEM((16, 16, HALF), BF),
             pltpu.VMEM((2, 96, HALF), BF),
             pltpu.VMEM((256, 128), BF),
+            pltpu.VMEM((16, 1536), BF),
+            pltpu.VMEM((2, 4, 4, 48, 64), F32),
             pltpu.VMEM((12, 256, HALF), BF),
             pltpu.VMEM((256, 2304), F32),
             pltpu.VMEM((12, 256, 2304), BF),
@@ -638,17 +645,6 @@
     )(*args)
 
 
-def allowed_row(tile_mask):
-    row, col = place()
-    r = row + jnp.arange(3, dtype=jnp.int32) - 1
-    s = col + jnp.arange(3, dtype=jnp.int32) - 1
-    rows = lax.axis_size("row")
-    cols = lax.axis_size("col")
-    inside = ((r >= 0) & (r < rows))[:, None] & ((s >= 0) & (s < cols))[None, :]
-    flags = jnp.where(inside.reshape(9) & (tile_mask.reshape(9) > 0), 1.0, 0.0).astype(F32)
-    return jnp.broadcast_to(jnp.repeat(flags, 256)[None], (8, 2304))
-
-
 def per_device(
     patch_tokens,
     queries,
@@ -660,20 +656,19 @@
     radius,
     tile_mask,
 ):
-    core = lax.rem(lax.axis_index("row"), 2)
     att, gd, gu = fused(
-        lax.dynamic_slice_in_dim(radius, core * 6, 6, 0).astype(F32),
+        radius,
+        tile_mask,
         queries.reshape(256, 1536),
         key_vectors.reshape(256, 1536),
         cotangent.reshape(256, 1536),
         patch_tokens.reshape(256, 3072),
-        jnp.pad(value_weight, ((0, 4), (0, 0))),
-        allowed_row(tile_mask),
-        jnp.pad(adapter_down, ((0, 0), (0, 64))),
-        lax.dynamic_slice_in_dim(adapter_up, core * HALF, HALF, 1),
+        value_weight,
+        adapter_down.T,
+        adapter_up,
         jnp.asarray(distances()),
     )
-    return att.reshape(16, 16, 1536), gd[:12], gu.reshape(1536, 64).T
+    return att.reshape(16, 16, 1536), gd, gu
 
 
 def solution(mesh):

time: 190 us -> 197 us (1.037)
  Pallas kernels: 177 us -> 191 us
  local copies, waits for them, and re-layouts: 10.1 us -> 5.13 us
  other arithmetic: 2.03 us -> 0 us
    pallas_call x1, Pallas kernels: 177 us -> 191 us  [fused(): pl.pallas_call(kernel, out_shape=[jax.ShapeDtypeStruct((256, 1536), BF),...]
    pad x2 -> x0, local copies, waits for them, and re-layouts: 2.46 us -> none  [the longest x1 1.42 us: per_device(): jnp.pad(value_weight, ((0, 4), (0, 0)))]
    reshape x1 -> x0, local copies, waits for them, and re-layouts: 2.14 us -> none  [per_device(): return (att.reshape(16, 16, 1536), gd[:12], gu.reshape(1536, 64).T)]
    unnamed x7 -> x3, local copies, waits for them, and re-layouts: 4.04 us -> 5.13 us
where the time goes in v4:
time: 197 us
  Pallas kernels  191 us (97%)
  local copies, waits for them, and re-layouts  5.13 us (3%)
    pallas_call x1, Pallas kernels, fused(): pl.pallas_call(kernel, out_shape=[jax.ShapeDtypeStruct((256, 1536), BF),...  191 us
    unnamed x3, local copies, waits for them, and re-layouts  5.13 us

profile of v4, /device:TPU:1, one launch (start us, length us, event | category | flops | bytes accessed | tf_op | source)
XLA Modules:
  0.0 197.2 jit_solution(13299521964825865999)
XLA Ops:
  0.6 191.4 %fused.1 = (bf16[256,1536]{1,0:T(8,128)(2,1)}, f32[12,64]{1,0:T(8,128)}, f32[64,1536]{1,0:T(8,128)}) custom-call(s32[12]{0:T(128)} %radius.1, s32[1,1,9]{2,1,0:T(1,128)} %mask.1, bf16[256,1536]{1,0:T(8,128)(2,1)} %bitcast.8, bf16[256,1536]{1,0:T(8,128)(2,1)} %bitcast.9, bf16[256,1536]{1,0:T(8,128)(2,1)} %bitcast.10, bf16[256,3072]{1,0:T(8,128)(2,1)} %bitcast.6, ...), custom_call_target="tpu_custom_call" | custom-call | tf_op jit(solution)/shard_map/fused/pallas_call | solution.py:591
  192.1 2.1 %copy.16 = bf16[16,16,1536]{2,1,0:T(8,128)(2,1)} copy(bf16[16,16,1536]{2,1,0:T(8,128)(2,1)} %bitcast.7) | data formatting | bytes 1572864
  194.1 1.3 copy.17
  195.4 1.8 copy.18

commit v5 on v4

--- a/solution.py
+++ b/solution.py
@@ -91,7 +91,7 @@
     radius, mask, q, kv, cot, x, w, down, up, dist,
     att, gd, gu,
     q2, kwin, c2, lwin, x2, wout, allow2, zbuf, wblk, low, wp, gun,
-    vwin, s_ref, p_ref, back, upt, att2,
+    vwin, s_one, s_two, p_ref, back, upt, att2,
     bs, br, gs, gr, keep, ux, uxr, ukeep, uy, uyr, uz, uzr, gx, gxr, gy, gyr, gz, gzr,
     send, recv, local,
 ):
@@ -157,20 +157,25 @@
 
     crossing = ((0, 1, 7, 15), (1, -1, 8, 0))
 
-    def side_sends(parts, win, rr, n, which):
+    def side_sends(parts, win, rr, n, which, far_ones):
         for h, target_core, src in parts:
             for i, d, hop, relay in crossing:
                 spot, near = win.at[rr * 3 + 1 - d], win.at[rr * 3 + 1 + d]
 
-                @pl.when((col != hop) & (col != relay))
-                def _(h=h, i=i, d=d, src=src, target_core=target_core, spot=spot):
-                    target = at_chip(k, target_core, col + d)
-                    wire.copy(src, spot, target, n + 2 * i + h, n + 2 * i + which).start()
-
-                @pl.when(col == hop)
-                def _(h=h, i=i, src=src, target_core=target_core, near=near, relay=relay):
-                    target = at_chip(k, target_core, jnp.int32(relay))
-                    wire.copy(src, near, target, n + 2 * i + h, n + 2 * (1 - i) + which).start()
+                if False in far_ones:
+
+                    @pl.when((col != hop) & (col != relay))
+                    def _(h=h, i=i, d=d, src=src, target_core=target_core, spot=spot):
+                        target = at_chip(k, target_core, col + d)
+                        wire.copy(src, spot, target, n + 2 * i + h, n + 2 * i + which).start()
+
+                if True in far_ones:
+
+                    @pl.when(col == hop)
+                    def _(h=h, i=i, src=src, target_core=target_core, near=near, relay=relay):
+                        target = at_chip(k, target_core, jnp.int32(relay))
+                        m = n + 2 * (1 - i) + which
+                        wire.copy(src, near, target, n + 2 * i + h, m).start()
 
     def side_relay(win, n):
         for i, d, hop, relay in crossing:
@@ -223,17 +228,21 @@
                 def _(n=n, i=i):
                     wire.copy(win.at[0], win.at[0], sib, n + i, n + i).wait_send()
 
-    def spread_tile(src, win, n, split):
-        part = lambda h: src.at[:, pl.ds(h * HALF, HALF)] if split else src
-        for h in (0, 1):
-            wire.start(part(h), win.at[far], at_chip(k + step, h, col), n + h, n + c)
-        side_sends([(h, h, part(h)) for h in (0, 1)], win, 1 + c, n + 2, c)
-        full = src.at[:, pl.ds(theirs, HALF)] if split else src
-        wire.start(full, win.at[centre], sib, n + 6, n + 6)
+    def halves(src, split):
+        return [src.at[:, pl.ds(h * HALF, HALF)] if split else src for h in (0, 1)]
+
+    def tile_up(src, win, n, split, by):
+        for h, part in enumerate(halves(src, split)):
+            by.start(part, win.at[far], at_chip(k + step, h, col), n + h, n + c)
+
+    def tile_sides(src, win, n, split, far_ones):
+        parts = [(h, h, part) for h, part in enumerate(halves(src, split))]
+        side_sends(parts, win, 1 + c, n, c, far_ones)
 
     for win in (kwin, lwin, vwin):
         clear_edges(win)
-    spread_tile(kv, kwin, 16, True)
+    tile_up(kv, kwin, 16, True, wire)
+    wire.start(kv.at[:, pl.ds(theirs, HALF)], kwin.at[centre], sib, 22, 22)
     wire.start(q.at[:, pl.ds(theirs, HALF)], q2.at[c], sib, 30, 30)
     wire.start(cot.at[:, pl.ds(theirs, HALF)], c2.at[c], sib, 31, 31)
     wire.start(x, x2.at[c], sib, 32, 32)
@@ -244,7 +253,7 @@
     ).astype(BF)
     low[:, 64:128] = jnp.zeros((256, 64), BF)
     lwin[centre] = low[...]
-    spread_tile(low, lwin, 23, False)
+    wire.start(low, lwin.at[centre], sib, 29, 29)
 
     locals_.pop().wait()
     wire.arrived(zbuf.at[0], 0)
@@ -310,18 +319,19 @@
         for i in (0, 1):
             sub.start(wblk, full(0, 0), one[i], w0 + i, w0 + i)
         across(0, wblk)
+        tile_sides(kv, kwin, 18, True, (False,))
         for i, d in enumerate((-1, 1)):
             sub.arrived(full(d, 0), w0 + i)
             sub.start(half(d, 0, i), half(d, 0, i), one[i], w0 + 2 + i, w0 + 2 + i)
             across(1 + i, full(d, 0))
+        tile_sides(kv, kwin, 18, True, (True,))
         corners(kwin, 16, 70)
-        side_relay(kwin, 18)
         pass_on(0)
         for i in (0, 1):
             sub.arrived(half(2, 0, i), w0 + 2 + i)
         across(3, full(2, 0))
-        corners(lwin, 23, 74)
-        side_relay(lwin, 25)
+        tile_up(low, lwin, 23, False, sub)
+        tile_sides(low, lwin, 25, False, (True, False))
         pass_on(1)
         pass_on(2)
         pass_on(3)
@@ -364,7 +374,11 @@
     wire.start(vwin.at[4], vwin.at[10], at_chip(k - 1, c, col), v0, v0)
     wire.start(vwin.at[7], vwin.at[1], at_chip(k + 1, c, col), v0 + 1, v0 + 1)
     for t in (0, 1):
-        side_sends([(t, c, vwin.at[4 + 3 * t])], vwin, 1 + t, v0 + 2, t)
+        side_sends([(t, c, vwin.at[4 + 3 * t])], vwin, 1 + t, v0 + 2, t, (True, False))
+
+    side_relay(kwin, 18)
+    corners(lwin, 23, 74)
+    side_relay(lwin, 25)
 
     side_arrivals(kwin, 18)
     side_arrivals(lwin, 25)
@@ -380,48 +394,62 @@
     back[...] = jnp.zeros_like(back)
     upt[...] = jnp.zeros_like(upt)
 
+    def place_of(i):
+        h, t = lax.div(i, 2), lax.rem(i, 2)
+        return h, t, pl.ds(pl.multiple_of(h * 128, 128), 128)
+
+    def score(i, to):
+        h, t, lanes = place_of(i)
+        keys = kwin[pl.ds(t * 3, 9), :, lanes].reshape(2304, 128)
+        to[...] = lax.dot_general(
+            q2[t, :, lanes], keys, (((1,), (1,)), ((), ())), preferred_element_type=F32
+        )
+
+    log_scale = 128**-0.5 * 1.4426950408889634
+
+    def soften(i, s_ref):
+        h, t, _ = place_of(i)
+        reach = radius[c * 6 + h]
+        limit = allow2[t, 0:1, :] * (reach * reach + 1).astype(F32) - 1.0
+        for j in range(8):
+            rows = slice(j * 32, (j + 1) * 32)
+            s = jnp.where(dist[rows] <= limit, s_ref[rows], -1e30)
+            e = jnp.exp2((s - jnp.max(s, axis=1, keepdims=True)) * log_scale)
+            p_ref[i, rows] = (e * (1.0 / jnp.sum(e, axis=1, keepdims=True))).astype(BF)
+
+    def gradient(i):
+        h, t, lanes = place_of(i)
+        vgt = jnp.dot(c2[t, :, lanes].T, p_ref[i], preferred_element_type=F32).astype(BF)
+        bt = jnp.dot(up[:, heads(h * 128, 128)], vgt, preferred_element_type=F32)
+        for n in range(9):
+            back[t * 3 + n] += bt[:, n * 256 : (n + 1) * 256]
+        lows = lwin[pl.ds(t * 3, 9)].reshape(2304, 128)
+        upt[lanes] += jnp.dot(vgt, lows, preferred_element_type=F32)
+
     def probs(lo, hi):
         @pl.loop(lo, hi)
-        def _(i):
-            h, t = lax.div(i, 2), lax.rem(i, 2)
-            lanes = pl.ds(pl.multiple_of(h * 128, 128), 128)
-            keys = kwin[pl.ds(t * 3, 9), :, lanes].reshape(2304, 128)
-            s_ref[...] = lax.dot_general(
-                q2[t, :, lanes], keys, (((1,), (1,)), ((), ())), preferred_element_type=F32
-            )
-            reach = radius[c * 6 + h]
-            limit = allow2[t, 0:1, :] * (reach * reach + 1).astype(F32) - 1.0
-
-            @pl.loop(0, 8)
-            def _(j):
-                rows = pl.ds(pl.multiple_of(j * 32, 32), 32)
-                s = jnp.where(dist[rows] <= limit, s_ref[rows] * 128**-0.5, -1e30)
-                e = jnp.exp(s - jnp.max(s, axis=1, keepdims=True))
-                p_ref[i, rows] = (e * (1.0 / jnp.sum(e, axis=1, keepdims=True))).astype(BF)
-
-            vgt = jnp.dot(c2[t, :, lanes].T, p_ref[i], preferred_element_type=F32).astype(BF)
-            bt = jnp.dot(up[:, heads(h * 128, 128)], vgt, preferred_element_type=F32)
-            for n in range(9):
-                back[t * 3 + n] += bt[:, n * 256 : (n + 1) * 256]
-            lows = lwin[pl.ds(t * 3, 9)].reshape(2304, 128)
-            rows = pl.ds(pl.multiple_of(h * 128, 128), 128)
-            upt[rows] += jnp.dot(vgt, lows, preferred_element_type=F32)
+        def _(m):
+            score(2 * m, s_one)
+            score(2 * m + 1, s_two)
+            soften(2 * m, s_one)
+            soften(2 * m + 1, s_two)
+            gradient(2 * m)
+            gradient(2 * m + 1)
 
     def attend(lo, hi):
-        @pl.loop(lo, hi)
-        def _(i):
-            h, t = lax.div(i, 2), lax.rem(i, 2)
-            lanes = pl.ds(pl.multiple_of(h * 128, 128), 128)
-            vals = vwin[pl.ds(t * 3, 9), :, lanes].reshape(2304, 128)
+        for i in range(lo, hi):
+            h, t = i // 2, i % 2
+            lanes = slice(h * 128, (h + 1) * 128)
+            vals = vwin[t * 3 : t * 3 + 9, :, lanes].reshape(2304, 128)
             att2[t, :, lanes] = jnp.dot(p_ref[i], vals, preferred_element_type=F32).astype(BF)
 
-    probs(0, 5)
+    probs(0, 4)
     wire.arrived(vwin.at[10], v0)
     corner(vwin, 60, 3)
     wire.arrived(vwin.at[1], v0 + 1)
     corner(vwin, 60, 0)
+    probs(4, 6)
     side_relay(vwin, v0 + 2)
-    probs(5, 12)
 
     def values_here():
         side_arrivals(vwin, v0 + 2)
@@ -611,6 +639,7 @@
             pltpu.VMEM((16, 1536), BF),
             pltpu.VMEM((2, 4, 4, 48, 64), F32),
             pltpu.VMEM((12, 256, HALF), BF),
+            pltpu.VMEM((256, 2304), F32),
             pltpu.VMEM((256, 2304), F32),
             pltpu.VMEM((12, 256, 2304), BF),
             pltpu.VMEM((12, 64, 256), F32),

time: 197 us -> 171 us (0.87)
  Pallas kernels: 191 us -> 164 us
    pallas_call x1, Pallas kernels: 191 us -> 164 us  [fused(): pl.pallas_call(kernel, out_shape=[jax.ShapeDtypeStruct((256, 1536), BF),...]
where the time goes in v5:
time: 171 us; the launch traced here: 170 us
  Pallas kernels  164 us (96%)
  local copies, waits for them, and re-layouts  5.13 us (3%)
    pallas_call x1, Pallas kernels, fused(): pl.pallas_call(kernel, out_shape=[jax.ShapeDtypeStruct((256, 1536), BF),...  164 us
    unnamed x3, local copies, waits for them, and re-layouts  5.13 us

profile of v5, /device:TPU:1, one launch (start us, length us, event | category | flops | bytes accessed | tf_op | source)
XLA Modules:
  0.0 170.3 jit_solution(13608569332740939328)
XLA Ops:
  0.6 164.5 %fused.1 = (bf16[256,1536]{1,0:T(8,128)(2,1)}, f32[12,64]{1,0:T(8,128)}, f32[64,1536]{1,0:T(8,128)}) custom-call(s32[12]{0:T(128)} %radius.1, s32[1,1,9]{2,1,0:T(1,128)} %mask.1, bf16[256,1536]{1,0:T(8,128)(2,1)} %bitcast.8, bf16[256,1536]{1,0:T(8,128)(2,1)} %bitcast.9, bf16[256,1536]{1,0:T(8,128)(2,1)} %bitcast.10, bf16[256,3072]{1,0:T(8,128)(2,1)} %bitcast.6, ...), custom_call_target="tpu_custom_call" | custom-call | tf_op jit(solution)/shard_map/fused/pallas_call | solution.py:619
  165.1 2.1 %copy.16 = bf16[16,16,1536]{2,1,0:T(8,128)(2,1)} copy(bf16[16,16,1536]{2,1,0:T(8,128)(2,1)} %bitcast.7) | data formatting | bytes 1572864
  167.2 1.3 copy.17
  168.5 1.8 %copy.18 = f32[64,1536]{1,0:T(8,128)} copy(f32[64,1536]{1,0:T(8,128)} %get-tuple-element.14) | data formatting | bytes 786432

commit v6 on v5

--- a/solution.py
+++ b/solution.py
@@ -10,6 +10,7 @@
 BF = jnp.bfloat16
 F32 = jnp.float32
 HALF = 768
+WIDE = 896
 MIB = 2**20
 
 
@@ -41,7 +42,7 @@
     barrier = pltpu.get_barrier_semaphore()
     for target in targets:
         pl.semaphore_signal(barrier, inc=1, device_id=target, device_id_type=MESH)
-    pl.semaphore_wait(barrier, len(targets))
+    return lambda: pl.semaphore_wait(barrier, len(targets))
 
 
 class Wire:
@@ -90,7 +91,7 @@
 def kernel(
     radius, mask, q, kv, cot, x, w, down, up, dist,
     att, gd, gu,
-    q2, kwin, c2, lwin, x2, wout, allow2, zbuf, wblk, low, wp, gun,
+    q2, kwin, c2, keys_out, x2, wout, allow2, zbuf, wblk, wp, gun,
     vwin, s_one, s_two, p_ref, back, upt, att2,
     bs, br, gs, gr, keep, ux, uxr, ukeep, uy, uyr, uz, uzr, gx, gxr, gy, gyr, gz, gzr,
     send, recv, local,
@@ -125,8 +126,90 @@
 
     slot = c * 8 + z
     centre = (1 + c) * 3 + 1
+    far = (3 - 3 * c) * 3 + 1
+    step = 2 * c - 1
+
+    crossing = ((0, 1, 7, 15), (1, -1, 8, 0))
+
+    def side_sends(parts, win, rr, n, which):
+        for h, target_core, src in parts:
+            for i, d, hop, relay in crossing:
+                spot, near = win.at[rr * 3 + 1 - d], win.at[rr * 3 + 1 + d]
+
+                @pl.when((col != hop) & (col != relay))
+                def _(h=h, i=i, d=d, src=src, target_core=target_core, spot=spot):
+                    target = at_chip(k, target_core, col + d)
+                    wire.copy(src, spot, target, n + 2 * i + h, n + 2 * i + which).start()
+
+                @pl.when(col == hop)
+                def _(h=h, i=i, src=src, target_core=target_core, near=near, relay=relay):
+                    target = at_chip(k, target_core, jnp.int32(relay))
+                    wire.copy(src, near, target, n + 2 * i + h, n + 2 * (1 - i) + which).start()
+
+    def side_relay(win, n):
+        for i, d, hop, relay in crossing:
+
+            @pl.when(col == relay)
+            def _(i=i, d=d, hop=hop):
+                for t in (0, 1):
+                    spot, near = win.at[(1 + t) * 3 + 1 - d], win.at[(1 + t) * 3 + 1 + d]
+                    wire.arrived(near, n + 2 * (1 - i) + t)
+                    m = n + 2 * i + t
+                    wire.copy(near, spot, (row, jnp.int32(hop + d)), m, m).start()
+
+    def side_arrivals(win, n):
+        for i, edge in enumerate((0, 15)):
+
+            @pl.when(col != edge)
+            def _(i=i):
+                wire.arrived(win.at[0], n + 2 * i)
+                wire.arrived(win.at[0], n + 2 * i + 1)
+
+        for m in range(4):
+            wire.copy(win.at[0], win.at[0], sib, n + m, n + m).wait_send()
+
+    def clear_edges(win):
+        for edge, cc in ((0, 0), (15, 2)):
+
+            @pl.when(col == edge)
+            def _(cc=cc):
+                for rr in (0, 3):
+                    win[rr * 3 + cc] = jnp.zeros(win.shape[1:], win.dtype)
+
+    def corner(win, m, rr):
+        src = win.at[rr * 3 + 1]
+        for i, d, _, edge in crossing:
+
+            @pl.when(col != edge)
+            def _(i=i, d=d):
+                n = m + (2 if rr else 0) + i
+                wire.copy(src, win.at[rr * 3 + 1 - d], at_chip(k, c, col + d), n, n).start()
+
+    def corner_arrivals(win, m):
+        for n in (m, m + 2):
+            for i, edge in enumerate((0, 15)):
+
+                @pl.when(col != edge)
+                def _(n=n, i=i):
+                    wire.arrived(win.at[0], n + i)
+
+                @pl.when(col != 15 - edge)
+                def _(n=n, i=i):
+                    wire.copy(win.at[0], win.at[0], sib, n + i, n + i).wait_send()
+
+    def keys_up():
+        for h in (0, 1):
+            wire.start(keys_out.at[h], kwin.at[far], at_chip(k + step, h, col), 16 + h, 16 + c)
+
+    def keys_aside():
+        parts = [(h, h, keys_out.at[h]) for h in (0, 1)]
+        side_sends(parts, kwin, 1 + c, 18, c)
+
+    met = greet(targets)
     own_x = local_copy(x, x2.at[c])
-    local_copy(kv.at[:, pl.ds(mine, HALF)], kwin.at[centre])
+    own_k = local_copy(kv.at[:, pl.ds(mine, HALF)], kwin.at[centre, :, pl.ds(0, HALF)])
+    for h in (0, 1):
+        local_copy(kv.at[:, pl.ds(h * HALF, HALF)], keys_out.at[h, :, pl.ds(0, HALF)])
     local_copy(q.at[:, pl.ds(mine, HALF)], q2.at[c])
     local_copy(cot.at[:, pl.ds(mine, HALF)], c2.at[c])
     for n in range(9):
@@ -138,8 +221,20 @@
     wp[...] = jnp.dot(
         jnp.where(r_out == r_in, 1.0, 0.0).astype(BF), w[...], preferred_element_type=F32
     ).astype(BF)
-    local_copy(wp.at[:, pl.ds(mine, HALF)], zbuf.at[slot])
-    greet(targets)
+    own_w = local_copy(wp.at[:, pl.ds(mine, HALF)], zbuf.at[slot])
+    own_x.wait()
+    low = lax.dot_general(
+        x2[c], down[...], (((1,), (1,)), ((), ())), preferred_element_type=F32
+    ).astype(BF)
+    low = jnp.concatenate([low, jnp.zeros((256, 64), BF)], axis=1)
+    for h in (0, 1):
+        keys_out[h, :, HALF:WIDE] = low
+    clear_edges(kwin)
+    clear_edges(vwin)
+    kwin[centre, :, HALF:WIDE] = low
+    for copy in locals_[1:]:
+        copy.wait()
+    met()
 
     wire.start(wp.at[:, pl.ds(theirs, HALF)], zbuf.at[slot], sib, 0, 0)
     for a in range(1, 8):
@@ -152,110 +247,12 @@
                 2 * a + h,
                 2 * a + h,
             )
-    far = (3 - 3 * c) * 3 + 1
-    step = 2 * c - 1
-
-    crossing = ((0, 1, 7, 15), (1, -1, 8, 0))
-
-    def side_sends(parts, win, rr, n, which, far_ones):
-        for h, target_core, src in parts:
-            for i, d, hop, relay in crossing:
-                spot, near = win.at[rr * 3 + 1 - d], win.at[rr * 3 + 1 + d]
-
-                if False in far_ones:
-
-                    @pl.when((col != hop) & (col != relay))
-                    def _(h=h, i=i, d=d, src=src, target_core=target_core, spot=spot):
-                        target = at_chip(k, target_core, col + d)
-                        wire.copy(src, spot, target, n + 2 * i + h, n + 2 * i + which).start()
-
-                if True in far_ones:
-
-                    @pl.when(col == hop)
-                    def _(h=h, i=i, src=src, target_core=target_core, near=near, relay=relay):
-                        target = at_chip(k, target_core, jnp.int32(relay))
-                        m = n + 2 * (1 - i) + which
-                        wire.copy(src, near, target, n + 2 * i + h, m).start()
-
-    def side_relay(win, n):
-        for i, d, hop, relay in crossing:
-
-            @pl.when(col == relay)
-            def _(i=i, d=d, hop=hop):
-                for t in (0, 1):
-                    spot, near = win.at[(1 + t) * 3 + 1 - d], win.at[(1 + t) * 3 + 1 + d]
-                    wire.arrived(near, n + 2 * (1 - i) + t)
-                    m = n + 2 * i + t
-                    wire.copy(near, spot, (row, jnp.int32(hop + d)), m, m).start()
-
-    def side_arrivals(win, n):
-        for i, edge in enumerate((0, 15)):
-
-            @pl.when(col != edge)
-            def _(i=i):
-                wire.arrived(win.at[0], n + 2 * i)
-                wire.arrived(win.at[0], n + 2 * i + 1)
-
-        for m in range(4):
-            wire.copy(win.at[0], win.at[0], sib, n + m, n + m).wait_send()
-
-    def clear_edges(win):
-        for edge, cc in ((0, 0), (15, 2)):
-
-            @pl.when(col == edge)
-            def _(cc=cc):
-                for rr in (0, 3):
-                    win[rr * 3 + cc] = jnp.zeros(win.shape[1:], win.dtype)
-
-    def corner(win, m, rr):
-        src = win.at[rr * 3 + 1]
-        for i, d, _, edge in crossing:
-
-            @pl.when(col != edge)
-            def _(i=i, d=d):
-                n = m + (2 if rr else 0) + i
-                wire.copy(src, win.at[rr * 3 + 1 - d], at_chip(k, c, col + d), n, n).start()
-
-    def corner_arrivals(win, m):
-        for n in (m, m + 2):
-            for i, edge in enumerate((0, 15)):
-
-                @pl.when(col != edge)
-                def _(n=n, i=i):
-                    wire.arrived(win.at[0], n + i)
-
-                @pl.when(col != 15 - edge)
-                def _(n=n, i=i):
-                    wire.copy(win.at[0], win.at[0], sib, n + i, n + i).wait_send()
-
-    def halves(src, split):
-        return [src.at[:, pl.ds(h * HALF, HALF)] if split else src for h in (0, 1)]
-
-    def tile_up(src, win, n, split, by):
-        for h, part in enumerate(halves(src, split)):
-            by.start(part, win.at[far], at_chip(k + step, h, col), n + h, n + c)
-
-    def tile_sides(src, win, n, split, far_ones):
-        parts = [(h, h, part) for h, part in enumerate(halves(src, split))]
-        side_sends(parts, win, 1 + c, n, c, far_ones)
-
-    for win in (kwin, lwin, vwin):
-        clear_edges(win)
-    tile_up(kv, kwin, 16, True, wire)
-    wire.start(kv.at[:, pl.ds(theirs, HALF)], kwin.at[centre], sib, 22, 22)
+    keys_up()
+    wire.start(keys_out.at[other], kwin.at[centre], sib, 22, 22)
     wire.start(q.at[:, pl.ds(theirs, HALF)], q2.at[c], sib, 30, 30)
     wire.start(cot.at[:, pl.ds(theirs, HALF)], c2.at[c], sib, 31, 31)
     wire.start(x, x2.at[c], sib, 32, 32)
     wire.start(allow2.at[c], allow2.at[c], sib, 33, 33)
-    own_x.wait()
-    low[:, 0:64] = lax.dot_general(
-        x2[c], down[...], (((1,), (1,)), ((), ())), preferred_element_type=F32
-    ).astype(BF)
-    low[:, 64:128] = jnp.zeros((256, 64), BF)
-    lwin[centre] = low[...]
-    wire.start(low, lwin.at[centre], sib, 29, 29)
-
-    locals_.pop().wait()
     wire.arrived(zbuf.at[0], 0)
     for a in range(1, 8):
         for h in (0, 1):
@@ -267,9 +264,6 @@
         part = zbuf[pl.ds(cc * 8, 8)].reshape(128, HALF)
         wblk[cc] = jnp.dot(pick, part, preferred_element_type=F32).astype(BF)
 
-    xs = (at_grid(y, xx + 1, z, c), at_grid(y, xx - 1, z, c))
-    ys = (at_grid(y + 1, xx, z, c), at_grid(y - 1, xx, z, c))
-
     def x_part(i):
         i = lax.rem(i + 4, 4)
         return lax.div(i, 2), lax.rem(i, 2)
@@ -293,70 +287,118 @@
             wire.arrived(win.at[rr * 3 + 1], first)
             corner(win, m, rr)
 
-    def spread(along_x):
-        sub = Wire(send, recv)
-        w0 = 34
-        if along_x:
-            one, two = xs, ys
-            full = lambda a, b: small(y + b, xx + a)
-            half = lambda a, b, j: small_half(y + b, xx + a, j)
-        else:
-            one, two = ys, xs
-            full = lambda a, b: small(y + a, xx + b)
-            half = lambda a, b, j: small_half(y + a, xx + b, j)
-        at = (0, -1, 1, 2)
-
-        def across(n, src):
-            for i in (0, 1):
-                sub.start(src, full(at[n], 0), two[i], w0 + 4 + 2 * n + i, w0 + 4 + 2 * n + i)
-
-        def pass_on(n):
-            for i, d in enumerate((-1, 1)):
-                sub.arrived(full(at[n], d), w0 + 4 + 2 * n + i)
-                m = w0 + 12 + 2 * n + i
-                sub.start(half(at[n], d, i), half(at[n], d, i), two[i], m, m)
-
+    fx, fy = 1 - c, c
+    ring = Wire(send, recv)
+    one = [at_grid(y + d * fy, xx + d * fx, z, c) for d in (1, -1)]
+    two = [at_grid(y + d * fx, xx + d * fy, z, c) for d in (1, -1)]
+    w0 = 34
+    at = (0, -1, 1, 2)
+
+    def full(a, b):
+        return small(y + a * fy + b * fx, xx + a * fx + b * fy)
+
+    def half(a, b, j):
+        return small_half(y + a * fy + b * fx, xx + a * fx + b * fy, j)
+
+    def across(n, src):
         for i in (0, 1):
-            sub.start(wblk, full(0, 0), one[i], w0 + i, w0 + i)
-        across(0, wblk)
-        tile_sides(kv, kwin, 18, True, (False,))
+            m = w0 + 4 + 2 * n + i
+            ring.start(src, full(at[n], 0), two[i], m, m)
+
+    def pass_on(n):
         for i, d in enumerate((-1, 1)):
-            sub.arrived(full(d, 0), w0 + i)
-            sub.start(half(d, 0, i), half(d, 0, i), one[i], w0 + 2 + i, w0 + 2 + i)
-            across(1 + i, full(d, 0))
-        tile_sides(kv, kwin, 18, True, (True,))
-        corners(kwin, 16, 70)
-        pass_on(0)
-        for i in (0, 1):
-            sub.arrived(half(2, 0, i), w0 + 2 + i)
-        across(3, full(2, 0))
-        tile_up(low, lwin, 23, False, sub)
-        tile_sides(low, lwin, 25, False, (True, False))
-        pass_on(1)
-        pass_on(2)
-        pass_on(3)
-        for n in range(4):
-            for i in (0, 1):
-                sub.arrived(half(0, 2, i), w0 + 12 + 2 * n + i)
-        own_copy.wait()
-        sub.drain()
-
-    busy = lax.rem(z + 1, 8) < 2
-
-    @pl.when((c == 0) | busy)
-    def _():
-        spread(True)
-
-    @pl.when((c == 1) & jnp.logical_not(busy))
-    def _():
-        spread(False)
+            ring.arrived(full(at[n], d), w0 + 4 + 2 * n + i)
+            m = w0 + 12 + 2 * n + i
+            ring.start(half(at[n], d, i), half(at[n], d, i), two[i], m, m)
+
+    for i in (0, 1):
+        ring.start(wblk, full(0, 0), one[i], w0 + i, w0 + i)
+    across(0, wblk)
+    keys_aside()
+    for i, d in enumerate((-1, 1)):
+        ring.arrived(full(d, 0), w0 + i)
+        ring.start(half(d, 0, i), half(d, 0, i), one[i], w0 + 2 + i, w0 + 2 + i)
+        across(1 + i, full(d, 0))
+    corners(kwin, 16, 70)
+    pass_on(0)
+    for i in (0, 1):
+        ring.arrived(half(2, 0, i), w0 + 2 + i)
+    across(3, full(2, 0))
+    side_relay(kwin, 18)
+    pass_on(1)
 
     def heads(start, width):
         return pl.ds(pl.multiple_of(mine + start, 128), width)
 
+    def keys_here():
+        side_arrivals(kwin, 18)
+        wire.arrived(q2.at[0], 30)
+        wire.arrived(c2.at[0], 31)
+        wire.arrived(allow2.at[0], 33)
+        corner_arrivals(kwin, 70)
+
+    back[...] = jnp.zeros_like(back)
+    upt[...] = jnp.zeros_like(upt)
+
+    def place_of(i):
+        h, t = lax.div(i, 2), lax.rem(i, 2)
+        return h, t, pl.ds(pl.multiple_of(h * 128, 128), 128)
+
+    def score(i, to):
+        h, t, lanes = place_of(i)
+        keys = kwin[pl.ds(t * 3, 9), :, lanes].reshape(2304, 128)
+        to[...] = lax.dot_general(
+            q2[t, :, lanes], keys, (((1,), (1,)), ((), ())), preferred_element_type=F32
+        )
+
+    log_scale = 128**-0.5 * 1.4426950408889634
+
+    def soften(i, s_ref):
+        h, t, _ = place_of(i)
+        reach = radius[c * 6 + h]
+        limit = allow2[t, 0:1, :] * (reach * reach + 1).astype(F32) - 1.0
+        for j in range(8):
+            rows = slice(j * 32, (j + 1) * 32)
+            s = jnp.where(dist[rows] <= limit, s_ref[rows], -1e30)
+            e = jnp.exp2((s - jnp.max(s, axis=1, keepdims=True)) * log_scale)
+            p_ref[i, rows] = (e * (1.0 / jnp.sum(e, axis=1, keepdims=True))).astype(BF)
+
+    def gradient(i):
+        h, t, lanes = place_of(i)
+        vgt = jnp.dot(c2[t, :, lanes].T, p_ref[i], preferred_element_type=F32).astype(BF)
+        bt = jnp.dot(up[:, heads(h * 128, 128)], vgt, preferred_element_type=F32)
+        for n in range(9):
+            back[t * 3 + n] += bt[:, n * 256 : (n + 1) * 256]
+        lows = kwin[pl.ds(t * 3, 9), :, HALF:WIDE].reshape(2304, 128)
+        upt[lanes] += jnp.dot(vgt, lows, preferred_element_type=F32)
+
+    def probs(lo, hi):
+        @pl.loop(lo, hi)
+        def _(m):
+            score(2 * m, s_one)
+            score(2 * m + 1, s_two)
+            soften(2 * m, s_one)
+            soften(2 * m + 1, s_two)
+            gradient(2 * m)
+            gradient(2 * m + 1)
+
+    def attend(lo, hi):
+        for i in range(lo, hi):
+            h, t = i // 2, i % 2
+            lanes = slice(h * 128, (h + 1) * 128)
+            vals = vwin[t * 3 : t * 3 + 9, :, lanes].reshape(2304, 128)
+            att2[t, :, lanes] = jnp.dot(p_ref[i], vals, preferred_element_type=F32).astype(BF)
+
+    pass_on(2)
+    pass_on(3)
+    for n in range(4):
+        for i in (0, 1):
+            ring.arrived(half(0, 2, i), w0 + 12 + 2 * n + i)
+    own_copy.wait()
+
     wire.arrived(x2.at[0], 32)
-    wire.arrived(lwin.at[0], 29)
-    low2 = jnp.concatenate([lwin[4][:, :64], lwin[7][:, :64]], axis=0)
+    wire.arrived(kwin.at[0], 22)
+    low2 = jnp.concatenate([kwin[4, :, HALF : HALF + 64], kwin[7, :, HALF : HALF + 64]], axis=0)
 
     @pl.loop(0, 3)
     def _(n):
@@ -374,82 +416,15 @@
     wire.start(vwin.at[4], vwin.at[10], at_chip(k - 1, c, col), v0, v0)
     wire.start(vwin.at[7], vwin.at[1], at_chip(k + 1, c, col), v0 + 1, v0 + 1)
     for t in (0, 1):
-        side_sends([(t, c, vwin.at[4 + 3 * t])], vwin, 1 + t, v0 + 2, t, (True, False))
-
-    side_relay(kwin, 18)
-    corners(lwin, 23, 74)
-    side_relay(lwin, 25)
-
-    side_arrivals(kwin, 18)
-    side_arrivals(lwin, 25)
-    wire.arrived(kwin.at[0], 22)
-    wire.arrived(q2.at[0], 30)
-    wire.arrived(c2.at[0], 31)
-    wire.arrived(allow2.at[0], 33)
-    corner_arrivals(kwin, 70)
-    corner_arrivals(lwin, 74)
-    for copy in locals_[1:]:
-        copy.wait()
-
-    back[...] = jnp.zeros_like(back)
-    upt[...] = jnp.zeros_like(upt)
-
-    def place_of(i):
-        h, t = lax.div(i, 2), lax.rem(i, 2)
-        return h, t, pl.ds(pl.multiple_of(h * 128, 128), 128)
-
-    def score(i, to):
-        h, t, lanes = place_of(i)
-        keys = kwin[pl.ds(t * 3, 9), :, lanes].reshape(2304, 128)
-        to[...] = lax.dot_general(
-            q2[t, :, lanes], keys, (((1,), (1,)), ((), ())), preferred_element_type=F32
-        )
-
-    log_scale = 128**-0.5 * 1.4426950408889634
-
-    def soften(i, s_ref):
-        h, t, _ = place_of(i)
-        reach = radius[c * 6 + h]
-        limit = allow2[t, 0:1, :] * (reach * reach + 1).astype(F32) - 1.0
-        for j in range(8):
-            rows = slice(j * 32, (j + 1) * 32)
-            s = jnp.where(dist[rows] <= limit, s_ref[rows], -1e30)
-            e = jnp.exp2((s - jnp.max(s, axis=1, keepdims=True)) * log_scale)
-            p_ref[i, rows] = (e * (1.0 / jnp.sum(e, axis=1, keepdims=True))).astype(BF)
-
-    def gradient(i):
-        h, t, lanes = place_of(i)
-        vgt = jnp.dot(c2[t, :, lanes].T, p_ref[i], preferred_element_type=F32).astype(BF)
-        bt = jnp.dot(up[:, heads(h * 128, 128)], vgt, preferred_element_type=F32)
-        for n in range(9):
-            back[t * 3 + n] += bt[:, n * 256 : (n + 1) * 256]
-        lows = lwin[pl.ds(t * 3, 9)].reshape(2304, 128)
-        upt[lanes] += jnp.dot(vgt, lows, preferred_element_type=F32)
-
-    def probs(lo, hi):
-        @pl.loop(lo, hi)
-        def _(m):
-            score(2 * m, s_one)
-            score(2 * m + 1, s_two)
-            soften(2 * m, s_one)
-            soften(2 * m + 1, s_two)
-            gradient(2 * m)
-            gradient(2 * m + 1)
-
-    def attend(lo, hi):
-        for i in range(lo, hi):
-            h, t = i // 2, i % 2
-            lanes = slice(h * 128, (h + 1) * 128)
-            vals = vwin[t * 3 : t * 3 + 9, :, lanes].reshape(2304, 128)
-            att2[t, :, lanes] = jnp.dot(p_ref[i], vals, preferred_element_type=F32).astype(BF)
-
-    probs(0, 4)
+        side_sends([(t, c, vwin.at[4 + 3 * t])], vwin, 1 + t, v0 + 2, t)
+
+    keys_here()
+
+    probs(0, 6)
     wire.arrived(vwin.at[10], v0)
     corner(vwin, 60, 3)
     wire.arrived(vwin.at[1], v0 + 1)
     corner(vwin, 60, 0)
-    probs(4, 6)
-    side_relay(vwin, v0 + 2)
 
     def values_here():
         side_arrivals(vwin, v0 + 2)
@@ -477,6 +452,7 @@
     for i in range(3):
         wire.start(ux.at[lax.rem(xx + i + 1, 4)], uxr.at[i], xt[i], u0 + i, u0 + i)
 
+    side_relay(vwin, v0 + 2)
     total = back[(1 + c) * 3 + 1]
     wire.arrived(br.at[0], b0 + 2 + other)
     total = total + br[2 + other].astype(F32)
@@ -499,12 +475,11 @@
     for i in range(3):
         wire.start(uy.at[lax.rem(y + i + 1, 4)], uyr.at[i], yt[i], u0 + 3 + i, u0 + 3 + i)
 
-    @pl.loop(0, 8)
-    def _(i):
-        part = x2[c, :, pl.ds(pl.multiple_of(i * 384, 384), 384)]
+    for i in range(8):
+        part = x2[c, :, i * 384 : (i + 1) * 384]
         g = jnp.dot(both, part, preferred_element_type=F32)
         g = (g[:64] + g[64:]).T
-        yi, xhi = lax.div(i, 2), lax.rem(i, 2)
+        yi, xhi = i // 2, i % 2
         for cc in (0, 1):
             for xl in (0, 1):
                 rows = g[(cc * 2 + xl) * 96 : (cc * 2 + xl + 1) * 96]
@@ -531,6 +506,8 @@
             gx[a, b] = full.astype(BF)
     for i in range(3):
         wire.start(gx.at[lax.rem(xx + i + 1, 4)], gxr.at[i], xt[i], e0 + 1 + i, e0 + 1 + i)
+    values_here()
+    attend(0, 4)
 
     scale = 65536**-0.5
     for i in range(7):
@@ -553,14 +530,12 @@
         gy[b] = acc.astype(BF)
     for i in range(3):
         wire.start(gy.at[lax.rem(y + i + 1, 4)], gyr.at[i], yt[i], e0 + 4 + i, e0 + 4 + i)
+    attend(4, 8)
 
     for i in range(3):
         wire.arrived(spot, u0 + 13 + i)
     for i in range(3):
         wire.start(gun.at[c, xx], gun.at[c, xx], xt[i], u0 + 16 + i, u0 + 16 + i)
-
-    values_here()
-    attend(0, 6)
 
     for i in range(3):
         wire.arrived(gyr.at[0], e0 + 4 + i)
@@ -581,7 +556,7 @@
         wire.arrived(gun.at[c, xx], u0 + 16 + i)
     wire.start(gun.at[c], gun.at[c], sib, u0 + 19, u0 + 19)
 
-    attend(6, 12)
+    attend(8, 12)
     wire.start(att2.at[other], att.at[:, pl.ds(mine, HALF)], sib, e0 + 14, e0 + 14)
     keep_att = pltpu.make_async_copy(att2.at[c], att.at[:, pl.ds(mine, HALF)], local.at[6])
     keep_att.start()
@@ -600,6 +575,7 @@
     wire.arrived(att.at[:, pl.ds(mine, HALF)], e0 + 14)
     keep_att.wait()
     wire.copy(bs.at[0], bs.at[0], sib, b0 + 12, b0 + 12).wait_send()
+    ring.drain()
     wire.drain()
 
 
@@ -627,15 +603,14 @@
         out_specs=[hb, vm, vm],
         scratch_shapes=[
             pltpu.VMEM((2, 256, HALF), BF),
-            pltpu.VMEM((12, 256, HALF), BF),
+            pltpu.VMEM((12, 256, WIDE), BF),
             pltpu.VMEM((2, 256, HALF), BF),
-            pltpu.VMEM((12, 256, 128), BF),
+            pltpu.VMEM((2, 256, WIDE), BF),
             pltpu.VMEM((2, 256, 3072), BF),
             pltpu.VMEM((4, 2, 2, 2, 96, HALF), BF),
             pltpu.VMEM((2, 8, 2304), F32),
             pltpu.VMEM((16, 16, HALF), BF),
             pltpu.VMEM((2, 96, HALF), BF),
-            pltpu.VMEM((256, 128), BF),
             pltpu.VMEM((16, 1536), BF),
             pltpu.VMEM((2, 4, 4, 48, 64), F32),
             pltpu.VMEM((12, 256, HALF), BF),

time: 171 us -> 155 us (0.906)
  Pallas kernels: 164 us -> 149 us
    pallas_call x1, Pallas kernels: 164 us -> 149 us  [fused(): pl.pallas_call(kernel, out_shape=[jax.ShapeDtypeStruct((256, 1536), BF),...]
where the time goes in v6:
time: 155 us
  Pallas kernels  149 us (96%)
  local copies, waits for them, and re-layouts  5.13 us (3%)
    pallas_call x1, Pallas kernels, fused(): pl.pallas_call(kernel, out_shape=[jax.ShapeDtypeStruct((256, 1536), BF),...  149 us
    unnamed x3, local copies, waits for them, and re-layouts  5.13 us

profile of v6, /device:TPU:1, one launch (start us, length us, event | category | flops | bytes accessed | tf_op | source)
XLA Modules:
  0.0 154.9 jit_solution(2817526165341288734)
XLA Ops:
  0.6 149.2 %fused.1 = (bf16[256,1536]{1,0:T(8,128)(2,1)}, f32[12,64]{1,0:T(8,128)}, f32[64,1536]{1,0:T(8,128)}) custom-call(s32[12]{0:T(128)} %radius.1, s32[1,1,9]{2,1,0:T(1,128)} %mask.1, bf16[256,1536]{1,0:T(8,128)(2,1)} %bitcast.8, bf16[256,1536]{1,0:T(8,128)(2,1)} %bitcast.9, bf16[256,1536]{1,0:T(8,128)(2,1)} %bitcast.10, bf16[256,3072]{1,0:T(8,128)(2,1)} %bitcast.6, ...), custom_call_target="tpu_custom_call" | custom-call | tf_op jit(solution)/shard_map/fused/pallas_call | solution.py:595
  149.8 2.1 %copy.16 = bf16[16,16,1536]{2,1,0:T(8,128)(2,1)} copy(bf16[16,16,1536]{2,1,0:T(8,128)(2,1)} %bitcast.7) | data formatting | bytes 1572864
  151.9 1.3 copy.17
  153.2 1.8 %copy.18 = f32[64,1536]{1,0:T(8,128)} copy(f32[64,1536]{1,0:T(8,128)} %get-tuple-element.14) | data formatting | bytes 786432

commit v7 on v6

--- a/solution.py
+++ b/solution.py
@@ -108,7 +108,8 @@
     xt = [at_grid(y, xx + a, z, c) for a in (1, 2, 3)]
     yt = [at_grid(y + a, xx, z, c) for a in (1, 2, 3)]
     zt = [at_grid(y, xx, z + a, c) for a in range(1, 8)]
-    targets += xt + yt
+    xo = [at_grid(y, xx + a, z, other) for a in (1, 2, 3)]
+    targets += xt + yt + xo
     targets += [at_chip(k, h, col + d) for d in (7, 8, 9) for h in (0, 1)]
     for h in (0, 1):
         for d in (1, -1):
@@ -421,10 +422,6 @@
     keys_here()
 
     probs(0, 6)
-    wire.arrived(vwin.at[10], v0)
-    corner(vwin, 60, 3)
-    wire.arrived(vwin.at[1], v0 + 1)
-    corner(vwin, 60, 0)
 
     def values_here():
         side_arrivals(vwin, v0 + 2)
@@ -445,7 +442,11 @@
             target = at_chip(k + dk, h, col + cc - 1)
             wire.start(bs.at[n], br.at[slot + c], target, b0 + n, b0 + slot + c)
 
-    u0, e0 = 92, 116
+    wire.arrived(vwin.at[10], v0)
+    corner(vwin, 60, 3)
+    wire.arrived(vwin.at[1], v0 + 1)
+    corner(vwin, 60, 0)
+    u0, e0 = 92, 120
     for a in range(4):
         for b in range(4):
             ux[a, b] = upt[(a * 4 + b) * 48 : (a * 4 + b + 1) * 48, 0:64].astype(BF)
@@ -532,10 +533,24 @@
         wire.start(gy.at[lax.rem(y + i + 1, 4)], gyr.at[i], yt[i], e0 + 4 + i, e0 + 4 + i)
     attend(4, 8)
 
+    def att_part(p):
+        return pl.ds(pl.multiple_of(mine + p * 512, 256), 512 if p == 0 else 256)
+
+    def att_sends(p):
+        lanes = slice(0, 512) if p == 0 else slice(512, HALF)
+        m = e0 + 14 + p
+        wire.start(att2.at[other, :, lanes], att.at[:, att_part(p)], sib, m, m)
+        pltpu.make_async_copy(att2.at[c, :, lanes], att.at[:, att_part(p)], local.at[5 + p]).start()
+
+    att_sends(0)
+
     for i in range(3):
         wire.arrived(spot, u0 + 13 + i)
     for i in range(3):
-        wire.start(gun.at[c, xx], gun.at[c, xx], xt[i], u0 + 16 + i, u0 + 16 + i)
+        for h, target in enumerate((xt[i], xo[i])):
+            m = u0 + 16 + 2 * i + h
+            wire.start(gun.at[c, xx], gun.at[c, xx], target, m, m)
+    wire.start(gun.at[c, xx], gun.at[c, xx], sib, u0 + 22, u0 + 22)
 
     for i in range(3):
         wire.arrived(gyr.at[0], e0 + 4 + i)
@@ -552,14 +567,9 @@
     for i in range(7):
         wire.start(gz.at[lax.rem(z + i + 1, 8)], gzr.at[i], zt[i], e0 + 7 + i, e0 + 7 + i)
 
-    for i in range(3):
-        wire.arrived(gun.at[c, xx], u0 + 16 + i)
-    wire.start(gun.at[c], gun.at[c], sib, u0 + 19, u0 + 19)
 
     attend(8, 12)
-    wire.start(att2.at[other], att.at[:, pl.ds(mine, HALF)], sib, e0 + 14, e0 + 14)
-    keep_att = pltpu.make_async_copy(att2.at[c], att.at[:, pl.ds(mine, HALF)], local.at[6])
-    keep_att.start()
+    att_sends(1)
 
     for i in range(7):
         wire.arrived(gzr.at[0], e0 + 7 + i)
@@ -567,13 +577,16 @@
     for i in range(7):
         acc = acc + gzr[i].astype(F32)
     gd[...] = (acc * scale)[0:12]
-    wire.arrived(gun.at[c], u0 + 19)
+    for i in range(7):
+        wire.arrived(gun.at[c, xx], u0 + 16 + i)
     for cc in (0, 1):
         for i in (0, 2):
             lanes = pl.ds(cc * HALF + i * 192, 384)
             gu[:, lanes] = gun[cc, i : i + 2].reshape(384, 64).T
-    wire.arrived(att.at[:, pl.ds(mine, HALF)], e0 + 14)
-    keep_att.wait()
+    for p in (0, 1):
+        wire.arrived(att.at[:, att_part(p)], e0 + 14 + p)
+        lanes = slice(0, 512) if p == 0 else slice(512, HALF)
+        pltpu.make_async_copy(att2.at[c, :, lanes], att.at[:, att_part(p)], local.at[5 + p]).wait()
     wire.copy(bs.at[0], bs.at[0], sib, b0 + 12, b0 + 12).wait_send()
     ring.drain()
     wire.drain()
@@ -638,8 +651,8 @@
             pltpu.VMEM((3, 96, 64), BF),
             pltpu.VMEM((8, 16, 64), BF),
             pltpu.VMEM((7, 16, 64), BF),
-            pltpu.SemaphoreType.DMA((136,)),
-            pltpu.SemaphoreType.DMA((136,)),
+            pltpu.SemaphoreType.DMA((138,)),
+            pltpu.SemaphoreType.DMA((138,)),
             pltpu.SemaphoreType.DMA((8,)),
         ],
         compiler_params=pltpu.CompilerParams(

time: 155 us -> 154 us (level)
  no operation moved by 1% of the time
where the time goes in v7:
time: 154 us
  Pallas kernels  148 us (96%)
  local copies, waits for them, and re-layouts  5.13 us (3%)
    pallas_call x1, Pallas kernels, fused(): pl.pallas_call(kernel, out_shape=[jax.ShapeDtypeStruct((256, 1536), BF),...  148 us
    unnamed x3, local copies, waits for them, and re-layouts  5.13 us

profile of v7, /device:TPU:1, one launch (start us, length us, event | category | flops | bytes accessed | tf_op | source)
XLA Modules:
  0.0 153.8 jit_solution(7913526213604048197)
XLA Ops:
  0.6 148.0 %fused.1 = (bf16[256,1536]{1,0:T(8,128)(2,1)}, f32[12,64]{1,0:T(8,128)}, f32[64,1536]{1,0:T(8,128)}) custom-call(s32[12]{0:T(128)} %radius.1, s32[1,1,9]{2,1,0:T(1,128)} %mask.1, bf16[256,1536]{1,0:T(8,128)(2,1)} %bitcast.8, bf16[256,1536]{1,0:T(8,128)(2,1)} %bitcast.9, bf16[256,1536]{1,0:T(8,128)(2,1)} %bitcast.10, bf16[256,3072]{1,0:T(8,128)(2,1)} %bitcast.6, ...), custom_call_target="tpu_custom_call" | custom-call | tf_op jit(solution)/shard_map/fused/pallas_call | solution.py:608
  148.7 2.1 %copy.16 = bf16[16,16,1536]{2,1,0:T(8,128)(2,1)} copy(bf16[16,16,1536]{2,1,0:T(8,128)(2,1)} %bitcast.7) | data formatting | bytes 1572864
  150.7 1.3 copy.17
  152.0 1.8 %copy.18 = f32[64,1536]{1,0:T(8,128)} copy(f32[64,1536]{1,0:T(8,128)} %get-tuple-element.14) | data formatting | bytes 786432

commit v8 on v7

--- a/solution.py
+++ b/solution.py
@@ -449,7 +449,7 @@
     u0, e0 = 92, 120
     for a in range(4):
         for b in range(4):
-            ux[a, b] = upt[(a * 4 + b) * 48 : (a * 4 + b + 1) * 48, 0:64].astype(BF)
+            ux[a, b // 2, :, (b % 2) * 64 : (b % 2) * 64 + 64] = upt[(a * 4 + b) * 48 : (a * 4 + b + 1) * 48, 0:64].astype(BF)
     for i in range(3):
         wire.start(ux.at[lax.rem(xx + i + 1, 4)], uxr.at[i], xt[i], u0 + i, u0 + i)
 
@@ -470,7 +470,7 @@
     for b in range(4):
         ua = upt[pl.ds(pl.multiple_of((xx * 4 + b) * 48, 16), 48), 0:64]
         for i in range(3):
-            ua = ua + uxr[i, b].astype(F32)
+            ua = ua + uxr[i, b // 2, :, (b % 2) * 64 : (b % 2) * 64 + 64].astype(F32)
         ukeep[b] = ua
         uy[b] = ua.astype(BF)
     for i in range(3):
@@ -504,7 +504,7 @@
         for b in range(4):
             full = keep[c, a, b] + gr[a, b].astype(F32)
             keep[0, a, b] = full
-            gx[a, b] = full.astype(BF)
+            gx[a, b // 2, :, (b % 2) * 64 : (b % 2) * 64 + 64] = full.astype(BF)
     for i in range(3):
         wire.start(gx.at[lax.rem(xx + i + 1, 4)], gxr.at[i], xt[i], e0 + 1 + i, e0 + 1 + i)
     values_here()
@@ -526,7 +526,7 @@
     for b in range(4):
         acc = keep[0, xx, b]
         for i in range(3):
-            acc = acc + gxr[i, b].astype(F32)
+            acc = acc + gxr[i, b // 2, :, (b % 2) * 64 : (b % 2) * 64 + 64].astype(F32)
         keep[1, 0, b] = acc
         gy[b] = acc.astype(BF)
     for i in range(3):
@@ -638,15 +638,15 @@
             pltpu.VMEM((2, 4, 4, 96, 64), BF),
             pltpu.VMEM((4, 4, 96, 64), BF),
             pltpu.VMEM((2, 4, 4, 96, 64), F32),
-            pltpu.VMEM((4, 4, 48, 64), BF),
-            pltpu.VMEM((3, 4, 48, 64), BF),
+            pltpu.VMEM((4, 2, 48, 128), BF),
+            pltpu.VMEM((3, 2, 48, 128), BF),
             pltpu.VMEM((4, 48, 64), F32),
             pltpu.VMEM((4, 48, 64), BF),
             pltpu.VMEM((3, 48, 64), BF),
             pltpu.VMEM((48, 64), BF),
             pltpu.VMEM((8, 48, 64), BF),
-            pltpu.VMEM((4, 4, 96, 64), BF),
-            pltpu.VMEM((3, 4, 96, 64), BF),
+            pltpu.VMEM((4, 2, 96, 128), BF),
+            pltpu.VMEM((3, 2, 96, 128), BF),
             pltpu.VMEM((4, 96, 64), BF),
             pltpu.VMEM((3, 96, 64), BF),
             pltpu.VMEM((8, 16, 64), BF),

time: 154 us -> 151 us (0.981)
  Pallas kernels: 148 us -> 145 us
    pallas_call x1, Pallas kernels: 148 us -> 145 us  [fused(): pl.pallas_call(kernel, out_shape=[jax.ShapeDtypeStruct((256, 1536), BF),...]
where the time goes in v8:
time: 151 us
  Pallas kernels  145 us (96%)
  local copies, waits for them, and re-layouts  5.13 us (3%)
    pallas_call x1, Pallas kernels, fused(): pl.pallas_call(kernel, out_shape=[jax.ShapeDtypeStruct((256, 1536), BF),...  145 us
    unnamed x3, local copies, waits for them, and re-layouts  5.13 us

profile of v8, /device:TPU:1, one launch (start us, length us, event | category | flops | bytes accessed | tf_op | source)
XLA Modules:
  0.0 151.0 jit_solution(6894318010200103346)
XLA Ops:
  0.6 145.2 %fused.1 = (bf16[256,1536]{1,0:T(8,128)(2,1)}, f32[12,64]{1,0:T(8,128)}, f32[64,1536]{1,0:T(8,128)}) custom-call(s32[12]{0:T(128)} %radius.1, s32[1,1,9]{2,1,0:T(1,128)} %mask.1, bf16[256,1536]{1,0:T(8,128)(2,1)} %bitcast.8, bf16[256,1536]{1,0:T(8,128)(2,1)} %bitcast.9, bf16[256,1536]{1,0:T(8,128)(2,1)} %bitcast.10, bf16[256,3072]{1,0:T(8,128)(2,1)} %bitcast.6, ...), custom_call_target="tpu_custom_call" | custom-call | tf_op jit(solution)/shard_map/fused/pallas_call | solution.py:608
  145.8 2.1 %copy.16 = bf16[16,16,1536]{2,1,0:T(8,128)(2,1)} copy(bf16[16,16,1536]{2,1,0:T(8,128)(2,1)} %bitcast.7) | data formatting | bytes 1572864
  147.9 1.3 copy.17
  149.2 1.8 %copy.18 = f32[64,1536]{1,0:T(8,128)} copy(f32[64,1536]{1,0:T(8,128)} %get-tuple-element.14) | data formatting | bytes 786432
